TPU v7x, 128 devices: a whole 4x4x4 slice. The times are simulated.
128 devices in a mesh: clip: 8 (over x, core), tile: 16 (over z, y).
Axes of the slice: x: 4, y: 4, z: 4, core: 2. Of those that a mesh axis runs over, the one named last changes fastest.
Arguments:
- latents: bfloat16 [32, 32, 2560], P('clip', 'tile'), may hold values from -6 to 6
- tile_route: int32 [32], replicated, may hold values from 0 to 31, as said below
- lengths: int32 [8], replicated, may hold values from 1 to 4, 20 in all
- reward_grad: bfloat16 [8, 4, 32, 160, 384], P('clip', None, 'tile'), may hold values from -6 to 6
- in_kernel: bfloat16 [432, 384], replicated, may hold values from -0.3125 to 0.3125
- in_bias: float32 [384], replicated, may hold values from -4 to 4
- norm_gain: float32 [384], replicated, may hold values from 0.5 to 1.5
- kernel: bfloat16 [10368, 384], replicated, may hold values from -0.0625 to 0.0625
Outputs:
- latent_grad: bfloat16 [32, 32, 2560], P('clip', 'tile')
- weight_grad: float32 [384, 10368], P('tile', 'clip')
Inputs may be any that keep to these rules, and one draw needn't show every extreme that they name: A permutation: slot s holds the tile of clip tile_route[s] // 4, frame tile_route[s] % 4; the 4 slots of one index of clip (slots 4 i to 4 i + 3) belong to 4 different clips: slot 4 i + j holds a tile of clip (i + d_j) mod 8, for 4 different shifts d_j that are the same for every i.
All inputs are finite; a program needn't handle non-finite values.
Results may differ from a plain program's by a relative error of at most 0.005.
Values may be sent and summed in bfloat16 or wider, within the bound.
A program may use at most 192 MiB of HBM per device.

v0:
```python
import math

import jax
import jax.numpy as jnp
from jax import lax
from jax.sharding import PartitionSpec as P

EPS = 1e-06


def with_halo(value, sides, width):
    for axis, dim in sides:
        count, length = (lax.axis_size(axis), value.shape[dim])
        up = [(i, (i + 1) % count) for i in range(count - 1)]
        down = [(j, i) for i, j in up]
        last = lax.slice_in_dim(value, length - width, length, axis=dim)
        initial = lax.slice_in_dim(value, 0, width, axis=dim)
        before = lax.ppermute(last, axis, up)
        after = lax.ppermute(initial, axis, down)
        value = jnp.concatenate([before, value, after], axis=dim)
    return value


def taps(extended, weights, flipped):
    frame_count = extended.shape[0]
    row_count = extended.shape[1] - 2
    col_count = extended.shape[2]
    channels = extended.shape[3]
    if flipped:
        padded = jnp.pad(extended, ((0, 2), (0, 0), (1, 1), (0, 0)))
        in_width = weights.shape[0] // 27
    else:
        padded = jnp.pad(extended, ((2, 0), (0, 0), (1, 1), (0, 0)))
        in_width = channels
    total = None
    for tap_index in range(27):
        delta_t, delta_y, delta_x = (tap_index // 9, tap_index // 3 % 3, tap_index % 3)
        block_rows = weights[tap_index * in_width : (tap_index + 1) * in_width]
        if flipped:
            window = padded[
                2 - delta_t : 2 - delta_t + frame_count,
                2 - delta_y : 2 - delta_y + row_count,
                2 - delta_x : 2 - delta_x + col_count,
            ]
            product = lax.dot_general(
                window.reshape(-1, channels),
                block_rows,
                (((1,), (1,)), ((), ())),
                preferred_element_type=jnp.float32,
            )
        else:
            window = padded[
                delta_t : delta_t + frame_count,
                delta_y : delta_y + row_count,
                delta_x : delta_x + col_count,
            ]
            product = jnp.dot(
                window.reshape(-1, channels), block_rows, preferred_element_type=jnp.float32
            )
        total = product if total is None else total + product
    return total.reshape(frame_count, row_count, col_count, -1)


def tap_products(extended, cotangent):
    leading = extended.ndim - 4
    padding = [(0, 0)] * leading + [(2, 0), (0, 0), (1, 1), (0, 0)]
    padded = jnp.pad(extended, padding)
    frame_count, row_count, col_count = (
        cotangent.shape[-4],
        cotangent.shape[-3],
        cotangent.shape[-2],
    )
    flat_cot = cotangent.reshape(-1, cotangent.shape[-1])
    products = []
    for tap_index in range(27):
        delta_t, delta_y, delta_x = (tap_index // 9, tap_index // 3 % 3, tap_index % 3)
        window = padded[
            ...,
            delta_t : delta_t + frame_count,
            delta_y : delta_y + row_count,
            delta_x : delta_x + col_count,
            :,
        ]
        products.append(
            lax.dot_general(
                window.reshape(-1, padded.shape[-1]),
                flat_cot,
                (((0,), (0,)), ((), ())),
                preferred_element_type=jnp.float32,
            )
        )
    return jnp.concatenate(products, axis=1)


def norm_backward(act_grad, hidden, normed, inv_rms, norm_gain):
    sigmoid_n = jax.nn.sigmoid(normed)
    gained = act_grad * sigmoid_n * (1.0 + normed * (1.0 - sigmoid_n)) * norm_gain
    inner = jnp.mean(gained * hidden, axis=-1, keepdims=True)
    return (inv_rms * gained - hidden * inv_rms * inv_rms * inv_rms * inner).astype(jnp.bfloat16)


def on_device(latents, tile_route, lengths, reward_grad, in_kernel, in_bias, norm_gain, kernel):
    frames, row_count, merged = latents.shape
    channels = kernel.shape[1]
    latent_ch = in_kernel.shape[0] // 27
    col_count = merged // latent_ch
    clip_count = lax.axis_size("clip")
    groups = lax.axis_size("tile")
    clip_id = lax.axis_index("clip")
    frame_ids = jnp.arange(frames, dtype=jnp.int32)
    live_len = lax.dynamic_index_in_dim(lengths, clip_id, 0, keepdims=False)
    live_mask = (frame_ids < live_len).astype(jnp.bfloat16)
    placement = (tile_route[None, :] == (clip_id * frames + frame_ids)[:, None]).astype(
        jnp.bfloat16
    )
    gathered = lax.all_gather(latents, "clip", axis=0, tiled=True)
    arrived = jnp.einsum(
        "fs,srx->frx", placement, gathered, preferred_element_type=jnp.float32
    ).astype(jnp.bfloat16)
    masked = arrived * live_mask[:, None, None]
    lat_ext = with_halo(masked, (("tile", 1),), 1)
    hidden = (
        taps(lat_ext.reshape(frames, row_count + 2, col_count, latent_ch), in_kernel, False)
        + in_bias
    )
    inv_rms = lax.rsqrt(jnp.mean(hidden * hidden, axis=-1, keepdims=True) + EPS)
    normed = hidden * inv_rms * norm_gain
    activated = jax.nn.silu(normed).astype(jnp.bfloat16)
    live_cells = live_mask[:, None, None, None]
    cotangent = reward_grad[0] * live_cells
    stacked_pair = jnp.stack(
        [
            activated.reshape(frames, row_count, col_count * channels),
            cotangent.reshape(frames, row_count, col_count * channels),
        ]
    )
    pair_ext = with_halo(stacked_pair, (("tile", 2),), 1)
    act_ext = pair_ext[0].reshape(frames, row_count + 2, col_count, channels)
    cot_ext = pair_ext[1].reshape(frames, row_count + 2, col_count, channels)
    act_grad = taps(cot_ext, kernel, True)
    hid_grad = norm_backward(act_grad, hidden, normed, inv_rms, norm_gain)
    hid_ext = with_halo(
        hid_grad.reshape(frames, row_count, col_count * channels), (("tile", 1),), 1
    )
    lat_grad = taps(
        hid_ext.reshape(frames, row_count + 2, col_count, channels), in_kernel, True
    ) * live_cells.astype(jnp.float32)
    lat_grad = lat_grad.astype(jnp.bfloat16).reshape(frames, row_count, merged)
    spread = jnp.einsum("fs,frx->srx", placement, lat_grad, preferred_element_type=jnp.float32)
    returned = lax.psum_scatter(
        spread.astype(jnp.bfloat16), "clip", scatter_dimension=0, tiled=True
    )
    group_sum = lax.psum_scatter(
        tap_products(act_ext, cotangent), "tile", scatter_dimension=0, tiled=True
    )
    inv_root = 1.0 / math.sqrt(clip_count * frames * groups * row_count * col_count)
    weight_grad = lax.psum_scatter(group_sum, "clip", scatter_dimension=1, tiled=True) * inv_root
    return (returned, weight_grad)


def solution(mesh):
    return jax.shard_map(
        on_device,
        mesh=mesh,
        in_specs=(
            P("clip", "tile", None),
            P(),
            P(),
            P("clip", None, "tile", None, None),
            P(),
            P(),
            P(),
            P(),
        ),
        out_specs=(P("clip", "tile", None), P("tile", "clip")),
        check_vma=False,
    )
```

profile of v0, /device:TPU:0, one launch (start us, length us, event | category | flops | bytes accessed | tf_op | source)
XLA Modules:
  0.0 539.7 jit_solution(11280562559335323527)
XLA Ops:
  7.2 13.6 %all_gather.3 = bf16[32,2,2560]{2,1,0:T(2,128)(2,1)S(1)} all-gather(bf16[4,2,2560]{2,1,0:T(2,128)(2,1)} %param.8), channel_id=1, replica_groups=mesh['clip'=8,'tile'=16] {'clip'}, dimensions={0}, use_global_device_ids=true | all-gather | bytes 368640 | tf_op jit(solution)/shard_map/all_gather | solution.py:116
  24.9 4.5 collective-permute-start
  29.5 2.2 reshape.543
  34.2 2.5 pad_slice_fusion.48
  47.6 1.7 mul.243
  49.3 4.3 reshape.542
  53.6 2.7 reshape.454
  56.3 5.6 %fusion.19 = bf16[1,4,2,61440]{3,1,2,0:T(4,128)(2,1)S(1)} fusion(f32[1,4,2,61440]{3,2,1,0:T(2,128)} %reshape.542, f32[1,4,2,61440]{3,2,1,0:T(2,128)} %reshape.454, f32[61440]{0:T(1024)S(1)} %mul.248, f32[61440]{0:T(1024)S(1)} %add.379), kind=kLoop, calls=%fused_computation.188 | loop fusion | flops 3932160 | bytes 5406720 | tf_op jit(solution)/shard_map/convert_element_type | solution.py:128
  62.0 2.5 fusion.47
  65.8 5.5 %collective-permute-start.2 = (bf16[2,4,1,61440]{3,1,2,0:T(4,128)(2,1)}, bf16[2,4,1,61440]{3,1,2,0:T(4,128)(2,1)}, u32[]{:S(2)}, u32[]{:S(2)}) collective-permute-start(bf16[2,4,1,61440]{3,1,2,0:T(4,128)(2,1)} %get-tuple-element.63), channel_id=1, source_target_pairs={{0,1},{1,2},{2,3},{3,4},{4,5},{5,6},{6,7},{7,8},{8,9},{9,10},{10,1... | collective-permute-start | bytes 2949128 | tf_op jit(solution)/shard_map/ppermute | solution.py:18
  73.3 2.5 reshape.483
  75.8 4.4 reshape.541
  80.2 9.9 %collective-permute-done.3 = bf16[2,4,1,61440]{3,1,2,0:T(4,128)(2,1)} collective-permute-done((bf16[2,4,1,61440]{3,1,2,0:T(4,128)(2,1)}, bf16[2,4,1,61440]{3,1,2,0:T(4,128)(2,1)}, u32[]{:S(2)}, u32[]{:S(2)}) %collective-permute-start.3) | collective-permute-done | bytes 983072 | tf_op jit(solution)/shard_map/ppermute | solution.py:19
  91.3 4.9 pad_maximum_fusion
  96.2 2.7 fusion.170
  98.9 3.1 reshape.544
  101.9 3.1 fusion.173
  105.0 5.3 pad_slice_fusion.24
  110.4 2.0 fusion.75
  133.0 2.8 multiply_reduce_fusion
  135.9 1.5 mul.273
  137.5 4.4 reshape.545
  141.8 4.3 reshape.482
  146.1 4.5 reshape.546
  150.7 2.9 fusion.43
  153.6 1.7 fusion.42
  155.3 1.7 fusion.41
  157.0 1.7 fusion.40
  158.7 1.7 fusion.39
  160.4 1.7 fusion.38
  162.1 1.7 fusion.37
  163.8 1.7 fusion.36
  165.4 1.7 fusion.35
  167.1 1.7 fusion.34
  168.9 1.7 fusion.33
  170.5 1.7 fusion.32
  172.3 1.7 fusion.31
  174.0 1.7 fusion.30
  175.6 1.7 fusion.29
  177.4 1.8 fusion.28
  179.1 1.7 fusion.27
  180.8 1.7 fusion.26
  182.5 2.1 fusion.25
  184.7 1.7 fusion.46
  186.3 1.7 fusion.24
  188.0 1.7 fusion.23
  189.8 1.7 fusion.45
  191.5 1.7 fusion.22
  193.2 1.7 fusion.21
  194.9 1.7 fusion.44
  196.6 1.7 fusion.20
  198.4 10.2 %fusion.13 = bf16[4,2,61440]{2,0,1:T(4,128)(2,1)S(1)} fusion(f32[4,2,61440]{2,1,0:T(2,128)} %reshape.545, f32[4,2,61440]{2,1,0:T(2,128)} %reshape.482, f32[4,2,61440]{2,1,0:T(2,128)} %reshape.483, f32[4,2,61440]{2,1,0:T(2,128)} %reshape.541, f32[61440]{0:T(1024)S(1)} %mul.248, f32[61440]{0:T(1024)S(1)} %add.379), kind=kLoop, calls=%fused_computation.171 | loop fusion | flops 8847360 | bytes 9338880 | tf_op jit(solution)/shard_map/convert_element_type | solution.py:99
  210.4 5.0 collective-permute-start.4
  215.5 1.6 subtract_convert_fusion.1
  217.0 17.0 %collective-permute-done.5 = bf16[4,1,61440]{2,0,1:T(4,128)(2,1)S(1)} collective-permute-done((bf16[4,1,61440]{2,0,1:T(4,128)(2,1)S(1)}, bf16[4,1,61440]{2,0,1:T(4,128)(2,1)S(1)}, u32[]{:S(2)}, u32[]{:S(2)}) %collective-permute-start.5) | collective-permute-done | bytes 491552 | tf_op jit(solution)/shard_map/ppermute | solution.py:19
  234.1 2.6 collective-permute-done.4
  238.2 2.4 fusion.8
  243.5 6.1 %fusion.171 = (bf16[4,2,160,384]{3,2,1,0:T(8,128)(2,1)S(1)}, bf16[4,2,160,384]{3,2,1,0:T(8,128)(2,1)S(1)}, bf16[4,2,160,384]{3,2,1,0:T(8,128)(2,1)S(1)}, bf16[4,...) fusion(bf16[6,4,162,384]{3,2,1,0:T(8,128)(2,1)S(1)} %fusion.8), kind=kLoop, calls=%fused_computation.383 | loop fusion | bytes 37355520 | tf_op jit(solution)/shard_map/slice | solution.py:40
  249.6 1.8 convolution_add_fusion.73
  251.5 1.7 convolution_add_fusion.72
  264.7 162.5 %all-reduce.11.cloned.1.call-done = f32[384,10368]{0,1:T(8,128)} async-done(((f32[384,10368]{0,1:T(8,128)}), f32[384,10368]{0,1:T(8,128)}) %all-reduce.11.cloned.1.call-update) | async-done | bytes 15925264
  427.2 6.4 %constant_dynamic-slice_fusion = f32[24,10368]{0,1:T(8,128)} fusion(f32[384,10368]{0,1:T(8,128)} %all-reduce.11.cloned.1.call-done, u32[]{:T(128)S(6)} %multiply.20), kind=kLoop, calls=%fused_computation.351 | loop fusion | bytes 1990660
  435.5 53.6 %all-reduce.9.cloned.1.call-done = bf16[32,2,2560]{2,0,1:T(8,128)(2,1)} async-done(((bf16[32,2,2560]{2,0,1:T(8,128)(2,1)}), bf16[32,2,2560]{2,0,1:T(8,128)(2,1)}) %all-reduce.9.cloned.1.call-update) | async-done | bytes 327696
  490.7 40.2 %reduce-scatter.4.cloned.1.call-done = f32[24,1296]{0,1:T(8,128)} async-done(((f32[24,10368]{0,1:T(8,128)}), f32[24,1296]{0,1:T(8,128)}) %reduce-scatter.4.cloned.1.call-update) | async-done | bytes 124432 | tf_op jit(solution)/shard_map/reduce_scatter | solution.py:157
  (180 shorter events, 64.2 us)
Async XLA Ops:
  7.2 420.1 %all-reduce.11.cloned.1.call-start = ((), (), s32[]{:S(2)}) async-start(), calls=%async_computation.3 | async-start | bytes 31850496
  22.7 6.8 %copy-start.22 = (s32[4]{0:T(128)}, s32[4]{0:T(128)S(1)}, u32[]{:S(2)}) copy-start(s32[4]{0:T(128)S(1)} %iota_add_fusion) | copy-start | bytes 52
  23.6 9.5 %collective-permute-start.1 = (bf16[4,1,2560]{2,0,1:T(4,128)(2,1)S(1)}, bf16[4,1,2560]{2,0,1:T(4,128)(2,1)S(1)}, u32[]{:S(2)}, u32[]{:S(2)}) collective-permute-start(bf16[4,1,2560]{2,0,1:T(4,128)(2,1)S(1)} %get-tuple-element.97), channel_id=1, source_target_pairs={{1,0},{2,1},{3,2},{4,3},{5,4},{6,5},{7,6},{8,7},{9,8},{10,9},{11,1... | collective-permute-start | bytes 61448 | tf_op jit(solution)/shard_map/ppermute | solution.py:19
  24.9 8.1 %copy-start.20 = (f32[384]{0:T(512)S(1)}, f32[384]{0:T(512)}, u32[]{:S(2)}) copy-start(f32[384]{0:T(512)} %param.14) | copy-start | bytes 4612
  24.9 8.1 %copy-start.19 = (f32[384]{0:T(512)S(1)}, f32[384]{0:T(512)}, u32[]{:S(2)}) copy-start(f32[384]{0:T(512)} %param.13) | copy-start | bytes 4612
  24.9 8.2 %collective-permute-start = (bf16[4,1,2560]{2,0,1:T(4,128)(2,1)S(1)}, bf16[4,1,2560]{2,0,1:T(4,128)(2,1)S(1)}, u32[]{:S(2)}, u32[]{:S(2)}) collective-permute-start(bf16[4,1,2560]{2,0,1:T(4,128)(2,1)S(1)} %get-tuple-element.96), channel_id=1, source_target_pairs={{0,1},{1,2},{2,3},{3,4},{4,5},{5,6},{6,7},{7,8},{8,9},{9,10},{10,1... | collective-permute-start | bytes 61448 | tf_op jit(solution)/shard_map/ppermute | solution.py:18
  34.2 2.6 copy-start.15
  47.5 25.8 %copy-start = (f32[1280,384]{1,0:T(8,128)}, f32[1280,384]{1,0:T(8,128)S(1)}, u32[]{:S(2)}) copy-start(f32[1280,384]{1,0:T(8,128)S(1)} %get-tuple-element.99) | copy-start | bytes 5898244
  62.0 2.5 copy-start.2
  62.0 9.3 %copy-start.25 = (u32[128]{0:T(128)S(1)}, u32[128]{0:T(128)}, u32[]{:S(2)}) copy-start(u32[128]{0:T(128)} %constant.47) | copy-start | bytes 1540
  64.5 25.7 %collective-permute-start.3 = (bf16[2,4,1,61440]{3,1,2,0:T(4,128)(2,1)}, bf16[2,4,1,61440]{3,1,2,0:T(4,128)(2,1)}, u32[]{:S(2)}, u32[]{:S(2)}) collective-permute-start(bf16[2,4,1,61440]{3,1,2,0:T(4,128)(2,1)} %get-tuple-element.64), channel_id=1, source_target_pairs={{1,0},{2,1},{3,2},{4,3},{5,4},{6,5},{7,6},{8,7},{9,8},{10,9},{11,1... | collective-permute-start | bytes 2949128 | tf_op jit(solution)/shard_map/ppermute | solution.py:19
  65.8 25.5 %collective-permute-start.2 = (bf16[2,4,1,61440]{3,1,2,0:T(4,128)(2,1)}, bf16[2,4,1,61440]{3,1,2,0:T(4,128)(2,1)}, u32[]{:S(2)}, u32[]{:S(2)}) collective-permute-start(bf16[2,4,1,61440]{3,1,2,0:T(4,128)(2,1)} %get-tuple-element.63), channel_id=1, source_target_pairs={{0,1},{1,2},{2,3},{3,4},{4,5},{5,6},{6,7},{7,8},{8,9},{9,10},{10,1... | collective-permute-start | bytes 2949128 | tf_op jit(solution)/shard_map/ppermute | solution.py:18
  75.8 15.5 %copy-start.3 = (bf16[1,4,2,61440]{3,1,2,0:T(4,128)(2,1)S(1)}, bf16[1,4,2,61440]{3,1,2,0:T(4,128)(2,1)}, u32[]{:S(2)}) copy-start(bf16[1,4,2,61440]{3,1,2,0:T(4,128)(2,1)} %copy-done.2) | copy-start | bytes 2949124
  101.9 8.4 %slice-start = ((s8[7962624]{0:T(1024)(128)(4,1)}), s8[4194304]{0:T(1024)(128)(4,1)S(1)}, s32[]{:S(2)}) async-start(s8[7962624]{0:T(1024)(128)(4,1)} %bitcast.401), calls=%async_computation.4 | async-start | bytes 8388608
  105.0 5.4 slice-start.1
  131.3 1.5 copy-start.1
  131.3 1.8 copy-start.18
  146.1 4.6 copy-start.17
  150.7 2.9 copy-start.14
  198.3 290.8 %all-reduce.9.cloned.1.call-start = ((), (), s32[]{:S(2)}) async-start(), calls=%async_computation.2 | async-start | bytes 655360
  208.6 6.8 %copy-start.4 = (f32[1280,384]{1,0:T(8,128)S(1)}, f32[1280,384]{1,0:T(8,128)}, u32[]{:S(2)}) copy-start(f32[1280,384]{1,0:T(8,128)} %get-tuple-element.101) | copy-start | bytes 5898244
  209.0 25.0 %collective-permute-start.5 = (bf16[4,1,61440]{2,0,1:T(4,128)(2,1)S(1)}, bf16[4,1,61440]{2,0,1:T(4,128)(2,1)S(1)}, u32[]{:S(2)}, u32[]{:S(2)}) collective-permute-start(bf16[4,1,61440]{2,0,1:T(4,128)(2,1)S(1)} %get-tuple-element.68), channel_id=1, source_target_pairs={{1,0},{2,1},{3,2},{4,3},{5,4},{6,5},{7,6},{8,7},{9,8},{10,9},{11,1... | collective-permute-start | bytes 1474568 | tf_op jit(solution)/shard_map/ppermute | solution.py:19
  210.4 26.2 %collective-permute-start.4 = (bf16[4,1,61440]{2,0,1:T(4,128)(2,1)S(1)}, bf16[4,1,61440]{2,0,1:T(4,128)(2,1)S(1)}, u32[]{:S(2)}, u32[]{:S(2)}) collective-permute-start(bf16[4,1,61440]{2,0,1:T(4,128)(2,1)S(1)} %get-tuple-element.67), channel_id=1, source_target_pairs={{0,1},{1,2},{2,3},{3,4},{4,5},{5,6},{6,7},{7,8},{8,9},{9,10},{10,1... | collective-permute-start | bytes 1474568 | tf_op jit(solution)/shard_map/ppermute | solution.py:18
  240.6 1.0 copy-start.16
  249.6 3.6 copy-start.11
  249.6 4.0 copy-start.10
  251.5 2.5 copy-start.9
  253.2 1.3 copy-start.8
  253.6 1.3 copy-start.7
  254.0 1.4 copy-start.6
  254.4 1.4 copy-start.5
  256.9 1.3 copy-start.13
  260.8 1.2 copy-start.12
  261.5 2.0 copy-start.21
  261.5 2.0 copy-start.23
  264.6 266.3 %reduce-scatter.4.cloned.1.call-start = ((), (), s32[]{:S(2)}) async-start(), calls=%async_computation.1 | async-start | bytes 5971968 | tf_op jit(solution)/shard_map/reduce_scatter | solution.py:157
  433.7 0.7 copy-start.24
Sparse Core Ops, SparseCore 0:
  198.4 228.7 all-reduce.10
  429.5 59.5 all-reduce.8
  491.6 39.2 reduce-scatter.3
where the time goes:
time: 550 us; the launch traced here: 540 us
  waiting for transfers between devices  287 us (52%)
  matrix products  98.6 us (18%)
  local copies, waits for them, and re-layouts  72.5 us (13%)
  other arithmetic  32.6 us (6%)
  starting transfers between devices  19.2 us (3%)
  between operations  16.2 us (3%)
  blocking collectives  13.6 us (2%)
    unnamed x5, waiting for transfers between devices  216 us
    dot_general x27, matrix products, tap_products(): lax.dot_general(window.reshape(-1, padded.shape[-1]), flat_cot, (((0,), (...  47.6 us
    reduce_scatter x1, waiting for transfers between devices, on_device(): lax.psum_scatter(group_sum, 'clip', scatter_dimension=1, tiled=True)  40.2 us
    dot_general x54, matrix products, taps(): lax.dot_general(window.reshape(-1, channels), block_rows, (((1,), (1,)),...  38.4 us
    ppermute x3, waiting for transfers between devices, with_halo(): after = lax.ppermute(initial, axis, down)  26.9 us
    slice x4, local copies, waits for them, and re-layouts, taps(): padded[2 - delta_t:2 - delta_t + frame_count, 2 - delta_y:2 - delta_y + r...  15.4 us
    ppermute x3, starting transfers between devices, with_halo(): before = lax.ppermute(last, axis, up)  15.1 us
    all_gather x1, blocking collectives, on_device(): gathered = lax.all_gather(latents, 'clip', axis=0, tiled=True)  13.6 us
  transfers between devices with their start and end apart: 9, of which 7 were waited for; matrix products, arithmetic and copies ran while one was open for 11% of the time, Pallas kernels for 0%

commit v1 on v0

v1 whole, which is shorter than its diff:
```python
import math

import jax
import jax.numpy as jnp
from jax import lax
from jax.experimental import pallas as pl
from jax.experimental.pallas import tpu as pltpu
from jax.sharding import PartitionSpec as P

EPS = 1e-06
F, R, W, C, LAT, H, CLIPS = 4, 2, 160, 384, 16, 32, 8
POS = F * R * W
LANES = 256
MESH = pl.DeviceIdType.MESH
BF, F32 = jnp.bfloat16, jnp.float32

WAVES = (
    ((1, 7), ((9, 2), (63, 8)), "zy"),
    ((4,), ((40, 5),), "zy"),
    ((0, 8), ((0, 9),), "yz"),
    ((2, 6), ((20, 7), (60, 3)), "zy"),
    ((3, 5), ((27, 4), (45, 6)), "yz"),
)
OWN = 44


def dot(a, b, ca, cb):
    return lax.dot_general(a, b, (((ca,), (cb,)), ((), ())), preferred_element_type=F32)


def sigmoid(v):
    return 1.0 / (1.0 + jnp.exp(-v))


def kernel(
    route, lengths, lat_in, cot_in, ink, bias, gain, ker_in,
    out_lat, out_wg,
    cotbuf, cot3, kbuf, latg, lat4, s3, xt, hid, act, inv_ref, ag, hg, yt, lg, lgr, latg2,
    gbuf, own, r1, r2, res, q1, qs, q2, fin, x1, xs, x2,
    local_sem, send_sem, recv_sem,
):
    clip, tile = lax.axis_index("clip"), lax.axis_index("tile")
    x, core = clip // 2, clip % 2
    z, y = tile // 4, tile % 4
    me = {"clip": clip, "tile": tile}

    def at(**kw):
        d = {**me, **kw}
        return (d["clip"], d["tile"])

    sib = at(clip=2 * x + 1 - core)
    xp, xm, xo = (at(clip=2 * ((x + k) % 4) + core) for k in (1, 3, 2))
    zp, zm = (at(tile=4 * ((z + k) % 4) + y) for k in (1, 3))
    yp, ym = (at(tile=4 * z + (y + k) % 4) for k in (1, 3))
    tp, tm = (at(tile=(tile + k) % 16) for k in (1, 15))
    peers = (sib, xp, xm, xo, zp, zm, yp, ym, tp, tm)

    copies = []

    def send(src, dst, device):
        n = len(copies)
        cp = pltpu.make_async_remote_copy(
            src_ref=src, dst_ref=dst, send_sem=send_sem.at[n], recv_sem=recv_sem.at[n],
            device_id=device, device_id_type=MESH,
        )
        copies.append(cp)
        cp.start()
        return cp

    load_cot = pltpu.make_async_copy(cot_in.at[0], cotbuf.at[:, 1:3], local_sem.at[0])
    load_cot.start()
    load_ker = pltpu.make_async_copy(ker_in, kbuf, local_sem.at[1])
    load_ker.start()

    barrier = pltpu.get_barrier_semaphore()
    for p in peers:
        pl.semaphore_signal(barrier, inc=1, device_id=p, device_id_type=MESH)
    pl.semaphore_wait(barrier, len(peers))

    lat_x = [send(lat_in, latg.at[clip], d) for d in (xp, xm, xo)]
    lat_s = [send(lat_in, latg.at[clip], sib)]
    halo = [
        send(cot_in.at[0, :, 0], cotbuf.at[:, 3], tm),
        send(cot_in.at[0, :, 1], cotbuf.at[:, 0], tp),
    ]
    latg[clip] = lat_in[...]

    length = lengths[clip]
    live = [jnp.where(f < length, 1.0, 0.0).astype(F32) for f in range(F)]
    top = jnp.where(tile > 0, 1.0, 0.0).astype(F32)
    bottom = jnp.where(tile < 15, 1.0, 0.0).astype(F32)
    edge = (top, 1.0, 1.0, bottom)

    def build_cot(rows):
        col = lax.broadcasted_iota(jnp.int32, (W, C), 0)
        for f in range(F):
            for r in rows:
                v = cotbuf[f, r].astype(F32) * (live[f] * edge[r])
                after = jnp.where(col == W - 1, 0.0, pltpu.roll(v, W - 1, 0))
                before = jnp.where(col == 0, 0.0, pltpu.roll(v, 1, 0))
                cot3[f, r, :, 0:C] = after.astype(BF)
                cot3[f, r, :, C : 2 * C] = v.astype(BF)
                cot3[f, r, :, 2 * C : 3 * C] = before.astype(BF)

    def window(dt, dy):
        return cot3[2 - dt : 4, 2 - dy : 4 - dy].reshape((dt + 2) * R * W, 3 * C)

    def act_grad_part(dt, dy, first):
        t0 = 9 * dt + 3 * dy
        taps = jnp.concatenate([kbuf[(t0 + d) * C : (t0 + d + 1) * C] for d in range(3)], axis=1)
        out = dot(taps, window(dt, dy), 1, 1)
        n = (dt + 2) * R * W
        if first:
            ag[...] = out
        else:
            ag[:, :n] += out

    load_cot.wait()
    build_cot((1, 2))

    for cp in lat_x:
        cp.wait_recv()
    for k in (3, 1, 2):
        src = latg.at[2 * ((x + k) % 4) + core]
        lat_s.append(send(src, src, sib))

    load_ker.wait()
    act_grad_part(2, 1, True)
    for cp in lat_s:
        cp.wait_recv()

    for f in range(F):
        slot = jnp.int32(0)
        for s in range(CLIPS * F):
            slot = jnp.where(route[s] == clip * F + f, s, slot)
        v = latg[slot // F, slot % F].astype(F32) * live[f]
        lat4[f, 1] = v[:LAT].astype(BF)
        lat4[f, 2] = v[LAT:].astype(BF)
    lat_h = [send(lat4.at[:, 1], lat4.at[:, 3], tm), send(lat4.at[:, 2], lat4.at[:, 0], tp)]
    act_grad_part(1, 1, False)
    act_grad_part(0, 1, False)
    for cp in lat_h:
        cp.wait_recv()

    for f in range(F):
        for r in range(4):
            v = lat4[f, r].astype(F32) * edge[r]
            s3[f, r, 0:LAT] = pltpu.roll(v, 1, 1).astype(BF)
            s3[f, r, LAT : 2 * LAT] = v.astype(BF)
            s3[f, r, 2 * LAT :] = pltpu.roll(v, LANES - 1, 1).astype(BF)
    for f in range(F):
        for r in range(R):
            for dt in range(3):
                for dy in range(3):
                    at_rows = slice((3 * dt + dy) * 48, (3 * dt + dy + 1) * 48)
                    at_cols = slice((2 * f + r) * W, (2 * f + r + 1) * W)
                    if f - 2 + dt >= 0:
                        xt[at_rows, at_cols] = s3[f - 2 + dt, r + dy, :, 0:W]
                    else:
                        xt[at_rows, at_cols] = jnp.zeros((48, W), BF)
    hid[...] = dot(ink[...], xt[...], 0, 0) + bias[...]

    def norm_step(n, carry):
        cols = pl.ds(pl.multiple_of(n * 128, 128), 128)
        h = hid[:, cols]
        inv = lax.rsqrt(jnp.mean(h * h, axis=0, keepdims=True) + EPS)
        normed = h * inv * gain[...]
        act[:, cols] = (normed * sigmoid(normed)).astype(BF)
        inv_ref[:, cols] = inv
        return carry

    lax.fori_loop(0, POS // 128, norm_step, 0)

    def weight_part(g, order):
        dt, dy = g // 3, g % 3
        out = dot(act[:, : (dt + 2) * R * W], window(dt, dy), 1, 0)
        for k in range(9):
            v = out[:, 128 * k : 128 * (k + 1)]
            if order == "yz":
                v = jnp.concatenate(
                    [v[24 * (4 * b + a) : 24 * (4 * b + a) + 24] for a in range(4) for b in range(4)], axis=0
                )
            gbuf[9 * g + k] = v.astype(BF)

    def pick(a, b):
        return jnp.where(core == 0, a, b)

    def wave_steps(ranges, order, off):
        total = sum(n for _, n in ranges)
        mine = pl.ds(off, total)
        if order == "zy":
            (a, ap, am), (b, bp, bm) = (z, zp, zm), (y, yp, ym)
        else:
            (a, ap, am), (b, bp, bm) = (y, yp, ym), (z, zp, zm)
        st = {}

        def rows_a(k):
            return 96 * ((a + k) % 4)

        def rows_b(k):
            q = (b + k) % 4
            return pl.multiple_of(48 * (q // 2) + 16 * (q % 2), 16)

        def s0():
            st["c"], at0 = [], off
            for first, n in ranges:
                mirror = 81 - first - n
                src = gbuf.at[pl.ds(pick(mirror, first), n)]
                st["c"].append(send(src, own.at[pl.ds(at0, n)], sib))
                at0 += n

        def s1():
            for cp in st["c"]:
                cp.wait_recv()
            at0 = off
            for first, n in ranges:
                start = pick(first, 81 - first - n)

                def body(k, carry, start=start, at0=at0):
                    own[at0 + k] = (own[at0 + k].astype(F32) + gbuf[start + k].astype(F32)).astype(BF)
                    return carry

                lax.fori_loop(0, n, body, 0)
                at0 += n
            r = pl.multiple_of(rows_a(2), 48)
            st["p1"] = send(own.at[mine, pl.ds(r, 48)], r1.at[mine, 0], ap)
            st["m1"] = send(own.at[mine, pl.ds(pl.multiple_of(r + 48, 48), 48)], r1.at[mine, 1], am)

        def s2():
            for side, k, shift, device in ((0, 1, 0, ap), (1, 3, 48, am)):
                st["pm"[side] + "1"].wait_recv()
                rows = pl.ds(pl.multiple_of(rows_a(k) + shift, 48), 48)

                def body(t, carry, rows=rows, side=side):
                    own[off + t, rows] = (own[off + t, rows].astype(F32) + r1[off + t, side].astype(F32)).astype(BF)
                    return carry

                lax.fori_loop(0, total, body, 0)
                st["pm"[side] + "2"] = send(
                    own.at[mine, pl.ds(pl.multiple_of(rows_a(k), 96), 96)], r2.at[mine, side], device
                )

        def s3_():
            st["p2"].wait_recv()
            st["m2"].wait_recv()
            rows = pl.ds(pl.multiple_of(rows_a(0), 96), 96)

            def body(t, carry):
                i = off + t
                res[i] = (own[i, rows].astype(F32) + r2[i, 0].astype(F32) + r2[i, 1].astype(F32)).astype(BF)
                return carry

            lax.fori_loop(0, total, body, 0)
            r = rows_b(2)
            st["p3"] = send(res.at[mine, pl.ds(r, 16)], q1.at[mine, 0], bp)
            st["m3"] = send(res.at[mine, pl.ds(pl.multiple_of(r + 16, 16), 16)], q1.at[mine, 1], bm)

        def s4():
            for side, k, device in ((0, 1, bp), (1, 3, bm)):
                st["pm"[side] + "3"].wait_recv()
                r = rows_b(k)
                half = pl.ds(pl.multiple_of(r + 16 * side, 16), 16)
                other = pl.ds(pl.multiple_of(r + 16 - 16 * side, 16), 16)

                def body(t, carry, half=half, other=other, side=side):
                    i = off + t
                    qs[i, side, 16 * side : 16 * side + 16] = (
                        res[i, half].astype(F32) + q1[i, side].astype(F32)
                    ).astype(BF)
                    qs[i, side, 16 - 16 * side : 32 - 16 * side] = res[i, other]
                    return carry

                lax.fori_loop(0, total, body, 0)
                st["pm"[side] + "4"] = send(qs.at[mine, side], q2.at[mine, side], device)

        def s5():
            st["p4"].wait_recv()
            st["m4"].wait_recv()
            rows = pl.ds(rows_b(0), 32)
            odd = (b % 2) == 1
            at0 = off
            for first, n in ranges:
                mirror = 81 - first - n
                place = pick(
                    11 * (first // 20) + first % 20, 11 * ((mirror - 10) // 20) + (mirror - 10) % 20
                )

                def body(t, carry, place=place, at0=at0):
                    i = at0 + t
                    v = res[i, rows].astype(F32) + q2[i, 0].astype(F32) + q2[i, 1].astype(F32)
                    v = jnp.where(odd, v[8:], v[:24])
                    fin[place + t] = jnp.concatenate([v, jnp.zeros((8, 128), F32)], axis=0).astype(BF)
                    return carry

                lax.fori_loop(0, n, body, 0)
                at0 += n

        return [s0, s1, s2, s3_, s4, s5]

    in_flight = []

    def advance():
        for steps in list(in_flight):
            steps.pop(0)()
            if not steps:
                in_flight.remove(steps)

    off = 0
    for w, (groups, ranges, order) in enumerate(WAVES):
        if w == 2:
            for cp in halo:
                cp.wait_recv()
            build_cot((0, 3))
        for g in groups:
            weight_part(g, order)
        advance()
        steps = wave_steps(ranges, order, off)
        steps.pop(0)()
        in_flight.append(steps)
        off += sum(n for _, n in ranges)

    act_grad_part(2, 0, False)
    act_grad_part(1, 0, False)
    advance()
    act_grad_part(0, 0, False)
    act_grad_part(2, 2, False)
    advance()
    act_grad_part(1, 2, False)
    act_grad_part(0, 2, False)
    advance()

    def grad_step(n, carry):
        cols = pl.ds(pl.multiple_of(n * 128, 128), 128)
        h, inv = hid[:, cols], inv_ref[:, cols]
        normed = h * inv * gain[...]
        s = sigmoid(normed)
        gained = ag[:, cols] * s * (1.0 + normed * (1.0 - s)) * gain[...]
        inner = jnp.mean(gained * h, axis=0, keepdims=True)
        hg[:, cols] = (inv * gained - h * (inv * inv * inv * inner)).astype(BF)
        return carry

    lax.fori_loop(0, POS // 128, grad_step, 0)
    yt[...] = dot(ink[...], hg[...], 1, 0)

    col = lax.broadcasted_iota(jnp.int32, (LAT, POS), 1) % W
    summed = []
    for g in range(9):
        base = 48 * g
        after = jnp.where(col == W - 1, 0.0, pltpu.roll(yt[base : base + LAT], POS - 1, 1))
        before = jnp.where(col == 0, 0.0, pltpu.roll(yt[base + 2 * LAT : base + 3 * LAT], 1, 1))
        summed.append(yt[base + LAT : base + 2 * LAT] + after + before)
    for f in range(F):
        for r in range(4):
            total = None
            for dt in range(3):
                for dy in range(3):
                    fh, rh = f + 2 - dt, r - dy
                    if fh < F and 0 <= rh < R:
                        p = (2 * fh + rh) * W
                        term = summed[3 * dt + dy][:, p : p + W]
                        total = term if total is None else total + term
            lg[f, r, :, 0:W] = total
            lg[f, r, :, W:] = jnp.zeros((LAT, LANES - W), F32)
    lg_h = [send(lg.at[:, 0], lgr.at[:, 1], tm), send(lg.at[:, 3], lgr.at[:, 0], tp)]
    advance()
    for cp in lg_h:
        cp.wait_recv()
    for f in range(F):
        first = (lg[f, 1] + lgr[f, 0] * top) * live[f]
        second = (lg[f, 2] + lgr[f, 1] * bottom) * live[f]
        latg2[clip, f] = jnp.concatenate([first, second], axis=0).astype(BF)
    back_x = [send(latg2.at[clip], latg2.at[clip], d) for d in (xp, xm, xo)]
    back_s = [send(latg2.at[clip], latg2.at[clip], sib)]
    advance()
    for cp in back_x:
        cp.wait_recv()
    for k in (3, 1, 2):
        src = latg2.at[2 * ((x + k) % 4) + core]
        back_s.append(send(src, src, sib))
    while in_flight:
        advance()

    def win(k):
        return pl.ds(11 * ((x + k) % 4), 11)

    p1 = send(fin.at[win(2), 0:16], x1.at[0], xp)
    m1 = send(fin.at[win(2), 16:32], x1.at[1], xm)
    for cp in back_s:
        cp.wait_recv()
    for j in range(F):
        v = route[clip * F + j]
        out_lat[j] = latg2[v // F, v % F]
    second = []
    for side, k, cp, device in ((0, 1, p1, xp), (1, 3, m1, xm)):
        cp.wait_recv()
        v = fin[win(k)].astype(F32)
        a, b = v[:, 0:16], v[:, 16:32]
        got = x1[side].astype(F32)
        a, b = (a + got, b) if side == 0 else (a, b + got)
        xs[side] = jnp.concatenate([a, b], axis=1).astype(BF)
        second.append(send(xs.at[side], x2.at[side], device))
    for cp in second:
        cp.wait_recv()
    v = fin[win(0)].astype(F32) + x2[0].astype(F32) + x2[1].astype(F32)
    v = v[:, :24] * (1.0 / math.sqrt(CLIPS * F * H * W))
    flat = jnp.concatenate([v[k] for k in range(11)], axis=1)
    out_wg[...] = pltpu.roll(flat, 11 * 128 - 16 * clip, 1)[:, :1296]

    for cp in copies:
        cp.wait_send()


def on_device(latents, tile_route, lengths, reward_grad, in_kernel, in_bias, norm_gain, kernel_):
    lat = latents.reshape(F, R, W, LAT).transpose(0, 1, 3, 2).reshape(F, R * LAT, W)
    lat = jnp.pad(lat, ((0, 0), (0, 0), (0, LANES - W)))
    vmem = pl.BlockSpec(memory_space=pltpu.VMEM)
    smem = pl.BlockSpec(memory_space=pltpu.SMEM)
    hbm = pl.BlockSpec(memory_space=pl.ANY)

    def v(*shape, dtype=BF):
        return pltpu.VMEM(shape, dtype)

    lat_grad, weight_grad = pl.pallas_call(
        kernel,
        out_shape=(
            jax.ShapeDtypeStruct((F, R * LAT, LANES), BF),
            jax.ShapeDtypeStruct((24, 1296), F32),
        ),
        in_specs=[smem, smem, vmem, hbm, vmem, vmem, vmem, hbm],
        out_specs=(vmem, vmem),
        scratch_shapes=[
            v(F, 4, W, C),
            v(F, 4, W, 3 * C),
            v(27 * C, C),
            v(CLIPS, F, R * LAT, LANES),
            v(F, 4, LAT, LANES),
            v(F, 4, 3 * LAT, LANES),
            v(27 * LAT, POS),
            v(C, POS, dtype=F32),
            v(C, POS),
            v(1, POS, dtype=F32),
            v(C, POS, dtype=F32),
            v(C, POS),
            v(27 * LAT, POS, dtype=F32),
            v(F, 4, LAT, LANES, dtype=F32),
            v(F, 2, LAT, LANES, dtype=F32),
            v(CLIPS, F, R * LAT, LANES),
            v(81, C, 128),
            v(OWN, C, 128),
            v(OWN, 2, 48, 128),
            v(OWN, 2, 96, 128),
            v(OWN, 96, 128),
            v(OWN, 2, 16, 128),
            v(OWN, 2, 32, 128),
            v(OWN, 2, 32, 128),
            v(OWN, 32, 128),
            v(2, 11, 16, 128),
            v(2, 11, 32, 128),
            v(2, 11, 32, 128),
            pltpu.SemaphoreType.DMA((2,)),
            pltpu.SemaphoreType.DMA((96,)),
            pltpu.SemaphoreType.DMA((96,)),
        ],
        compiler_params=pltpu.CompilerParams(
            collective_id=0, has_side_effects=True, vmem_limit_bytes=62 * 2**20
        ),
        name="backward",
    )(
        tile_route, lengths, lat, reward_grad, in_kernel,
        in_bias.reshape(C, 1), norm_gain.reshape(C, 1), kernel_,
    )
    lat_grad = lat_grad[:, :, :W].reshape(F, R, LAT, W).transpose(0, 1, 3, 2).reshape(F, R, W * LAT)
    return lat_grad, weight_grad


def solution(mesh):
    return jax.shard_map(
        on_device,
        mesh=mesh,
        in_specs=(
            P("clip", "tile", None),
            P(),
            P(),
            P("clip", None, "tile", None, None),
            P(),
            P(),
            P(),
            P(),
        ),
        out_specs=(P("clip", "tile", None), P("tile", "clip")),
        check_vma=False,
    )
```

time: 550 us -> 103 us (0.19); the launches traced: 540 us -> 102 us
  waiting for transfers between devices: 287 us -> 0 us
  matrix products: 98.6 us -> 0 us
  Pallas kernels: 0 us -> 93.3 us
  local copies, waits for them, and re-layouts: 72.5 us -> 8.41 us
  other arithmetic: 32.6 us -> 0 us
  starting transfers between devices: 19.2 us -> 0 us
  between operations: 16.2 us -> 0.65 us
  blocking collectives: 13.6 us -> 0 us
    unnamed x5 -> x0, waiting for transfers between devices: 216 us -> none
    dot_general x110 -> x0, matrix products: 98.6 us -> none  [the longest x27 47.6 us: tap_products(): lax.dot_general(window.reshape(-1, padded.shape[-1]), flat_cot, (((0,), (...]
    pallas_call x0 -> x1, Pallas kernels: none -> 93.3 us  [on_device(): pl.pallas_call(kernel, out_shape=(jax.ShapeDtypeStruct((F, R * LAT, LANES...]
    reduce_scatter x1 -> x0, waiting for transfers between devices: 40.2 us -> none  [on_device(): lax.psum_scatter(group_sum, 'clip', scatter_dimension=1, tiled=True)]
    ppermute x6 -> x0, waiting for transfers between devices: 30.6 us -> none  [the longest x3 26.9 us: with_halo(): after = lax.ppermute(initial, axis, down)]
    slice x9 -> x0, local copies, waits for them, and re-layouts: 21.4 us -> none  [the longest x4 15.4 us: taps(): padded[2 - delta_t:2 - delta_t + frame_count, 2 - delta_y:2 - delta_y + r...]
    ppermute x6 -> x0, starting transfers between devices: 19.1 us -> none  [the longest x3 15.1 us: with_halo(): before = lax.ppermute(last, axis, up)]
    convert_element_type x6 -> x0, other arithmetic: 18.8 us -> none  [the longest x2 11.8 us: norm_backward(): (inv_rms * gained - hidden * inv_rms * inv_rms * inv_rms * inner).astype(...]
  transfers between devices with their start and end apart: 9 -> 0, of which waited for: 7 -> 0; matrix products, arithmetic and copies ran while one was open for 11% -> 0% of each run, Pallas kernels for 0% -> 0%
where the time goes in v1:
time: 103 us; the launch traced here: 102 us
  Pallas kernels  93.3 us (91%)
  local copies, waits for them, and re-layouts  8.41 us (8%)
    pallas_call x1, Pallas kernels, on_device(): pl.pallas_call(kernel, out_shape=(jax.ShapeDtypeStruct((F, R * LAT, LANES...  93.3 us

profile of v1, /device:TPU:0, one launch (start us, length us, event | category | flops | bytes accessed | tf_op | source)
XLA Modules:
  0.0 102.4 jit_solution(7840006529604336125)
XLA Ops:
  0.6 1.0 %reshape.22 = bf16[4,2,160,16]{3,2,1,0:T(8,128)(2,1)S(1)} reshape(bf16[4,2,2560]{2,1,0:T(2,128)(2,1)} %param.8) | data formatting | bytes 81920 | tf_op jit(solution)/shard_map/reshape | solution.py:414
  1.7 0.2 copy.12
  1.9 0.7 pad.4.lat_in
  2.5 1.5 %reshape.28.bias = f32[384,1]{1,0:T(8,128)} reshape(f32[384]{0:T(512)} %param.13) | data formatting | bytes 3072 | tf_op jit(solution)/shard_map/reshape | solution.py:470
  4.0 1.5 %reshape.29.gain = f32[384,1]{1,0:T(8,128)} reshape(f32[384]{0:T(512)} %param.14) | data formatting | bytes 3072 | tf_op jit(solution)/shard_map/reshape | solution.py:470
  5.5 93.3 %backward.1 = (bf16[4,32,256]{2,1,0:T(8,128)(2,1)}, f32[24,1296]{1,0:T(8,128)}) custom-call(s32[32]{0:T(128)} %route.1, s32[8]{0:T(128)} %lengths.1, bf16[4,32,256]{2,1,0:T(8,128)(2,1)} %pad.4.lat_in, bf16[1,4,2,160,384]{4,3,2,1,0:T(8,128)(2,1)} %cot_in.1, bf16[432,384]{1,0:T(8,128)(2,1)} %ink.1, f32[384,1]{1,0:T(8,128)} %reshape.28.bias, ...), custom_call_target="tpu_custom_call" | custom-call | tf_op jit(solution)/shard_map/backward/pallas_call | solution.py:423
  98.8 1.0 %copy.15 = bf16[4,2,16,160]{2,3,1,0:T(8,128)(2,1)S(1)} copy(bf16[4,2,16,160]{3,2,1,0:T(8,128)(2,1)} %bitcast.10) | data formatting | bytes 81920 | tf_op jit(solution)/shard_map/reshape | solution.py:472
  99.8 1.0 reshape.27
  100.8 1.6 %copy.17 = f32[24,1296]{1,0:T(8,128)} copy(f32[24,1296]{1,0:T(8,128)} %get-tuple-element.9) | data formatting | bytes 248832

commit v2 on v1

v2 whole, which is shorter than its diff:
```python
import math

import jax
import jax.numpy as jnp
from jax import lax
from jax.experimental import pallas as pl
from jax.experimental.pallas import tpu as pltpu
from jax.sharding import PartitionSpec as P

EPS = 1e-06
F, R, W, C, LAT, H, CLIPS = 4, 2, 160, 384, 16, 32, 8
POS = F * R * W
LANES = 256
MESH = pl.DeviceIdType.MESH
BF, F32 = jnp.bfloat16, jnp.float32

WAVES = (
    ((1, 7), ((9, 2), (63, 8)), "zy"),
    ((4,), ((40, 5),), "zy"),
    ((0, 8), ((0, 9),), "yz"),
    ((2, 6), ((20, 7), (60, 3)), "zy"),
    ((3, 5), ((27, 4), (45, 6)), "yz"),
)
OWN = 44

SCHEDULE = (
    ("G", 1), ("G", 7), (0, 0), ("T", "halo"), ("G", 3), ("G", 5), (4, 0), (0, 1), ("G", 0), ("G", 8), (2, 0),
    ("G", 4), (1, 0), (4, 1), ("G", 2), (0, 2), ("G", 6), (3, 0), (2, 1), (1, 1), ("A", 6), (4, 2), ("A", 3),
    (3, 1), ("A", 0), (2, 2), (0, 3), ("A", 8), (1, 2), ("A", 5), ("A", 2), (3, 2), (4, 3), ("T", "hidden"),
    (1, 3), (2, 3), (3, 3), (0, 4), ("T", "clip"), (1, 4), (4, 4), ("T", "pass"), (3, 4), (2, 4), ("T", "x"),
    ("T", "out"),
)


def dot(a, b, ca, cb):
    return lax.dot_general(a, b, (((ca,), (cb,)), ((), ())), preferred_element_type=F32)


def sigmoid(v):
    return 1.0 / (1.0 + jnp.exp(-v))


def roll(v, shift):
    return pltpu.roll(v, shift % 128, 1) if shift % 128 else v


def pack(tiles, ref):
    rest = None
    for f in range(F):
        ref[f] = tiles[f][:, :128].astype(BF)
        part = roll(tiles[f][:, 128:], 32 * f)
        rest = part if rest is None else rest + part
    ref[F] = rest.astype(BF)


def unpack(ref, slot):
    owner, j = slot // F, slot % F
    rest = ref[owner, F].astype(F32)
    out = rest
    for k in range(1, F):
        out = jnp.where(j == k, roll(rest, -32 * k), out)
    out = jnp.where(lax.broadcasted_iota(jnp.int32, out.shape, 1) < 32, out, 0.0)
    return jnp.concatenate([ref[owner, j].astype(F32), out], axis=1)


def as_column(ref):
    return jnp.broadcast_to(ref[...].reshape(1, C), (8, C)).T[:, :1]


def kernel(
    route, lengths, lat_in, cot_in, ink, bias_in, gain_in, ker_in,
    out_lat, out_wg,
    cotbuf, cot3, kbuf, tr1, tr2, stage, latg, lat4, s3, xt, hid, act, inv_ref, ag, hg, yt, lg, lgr, latg2,
    gbuf, own, r1, r2, res, q, fin, xr,
    local_sem, send_sem, recv_sem,
):
    clip, tile = lax.axis_index("clip"), lax.axis_index("tile")
    x, core = clip // 2, clip % 2
    z, y = tile // 4, tile % 4
    me = {"clip": clip, "tile": tile}

    def at(**kw):
        d = {**me, **kw}
        return (d["clip"], d["tile"])

    sib = at(clip=2 * x + 1 - core)
    xp, xm, xo = (at(clip=2 * ((x + k) % 4) + core) for k in (1, 3, 2))
    zp, zm, zo = (at(tile=4 * ((z + k) % 4) + y) for k in (1, 3, 2))
    yp, ym, yo = (at(tile=4 * z + (y + k) % 4) for k in (1, 3, 2))
    tp, tm = (at(tile=(tile + k) % 16) for k in (1, 15))
    peers = (sib, xp, xm, xo, zp, zm, zo, yp, ym, yo, tp, tm)

    copies = []

    def send(src, dst, device):
        n = len(copies)
        cp = pltpu.make_async_remote_copy(
            src_ref=src, dst_ref=dst, send_sem=send_sem.at[n], recv_sem=recv_sem.at[n],
            device_id=device, device_id_type=MESH,
        )
        copies.append(cp)
        cp.start()
        return cp

    load_cot = pltpu.make_async_copy(cot_in.at[0], cotbuf.at[:, 1:3], local_sem.at[0])
    load_cot.start()
    load_ker = pltpu.make_async_copy(ker_in, kbuf, local_sem.at[1])
    load_ker.start()

    barrier = pltpu.get_barrier_semaphore()
    for p in peers:
        pl.semaphore_signal(barrier, inc=1, device_id=p, device_id_type=MESH)

    lane16 = lax.broadcasted_iota(jnp.int32, (20, 128), 1) // LAT
    flat = jnp.concatenate([lat_in[j].astype(F32) for j in range(F)], axis=0)
    for g in range(20):
        tr1[pl.ds(g, 8, stride=24), :] = flat[:, 128 * g : 128 * (g + 1)]
    tr2[W:] = jnp.zeros((LANES - W, 128), F32)
    for q8 in range(8):
        u = jnp.zeros((20, 128), F32)
        for jr in range(8):
            u = jnp.where(lane16 == jr, roll(tr1[jr * 24 : jr * 24 + 20], LAT * (jr - q8)), u)
        tr2[pl.ds(q8, 20, stride=8), :] = u
    pack(tr2[...].T.reshape(F, R * LAT, LANES), stage)

    pl.semaphore_wait(barrier, len(peers))

    lat_x = [send(stage, latg.at[clip], d) for d in (xp, xm, xo)]
    lat_s = [send(stage, latg.at[clip], sib)]
    halo = [
        send(cot_in.at[0, :, 0], cotbuf.at[:, 3], tm),
        send(cot_in.at[0, :, 1], cotbuf.at[:, 0], tp),
    ]
    latg[clip] = stage[...]

    length = lengths[clip]
    live = [jnp.where(f < length, 1.0, 0.0).astype(F32) for f in range(F)]
    top = jnp.where(tile > 0, 1.0, 0.0).astype(F32)
    bottom = jnp.where(tile < 15, 1.0, 0.0).astype(F32)
    edge = (top, 1.0, 1.0, bottom)

    def build_cot(rows):
        col = lax.broadcasted_iota(jnp.int32, (W, C), 0)
        for f in range(F):
            for r in rows:
                v = cotbuf[f, r].astype(F32) * (live[f] * edge[r])
                after = jnp.where(col == W - 1, 0.0, pltpu.roll(v, W - 1, 0))
                before = jnp.where(col == 0, 0.0, pltpu.roll(v, 1, 0))
                cot3[f, r, :, 0:C] = after.astype(BF)
                cot3[f, r, :, C : 2 * C] = v.astype(BF)
                cot3[f, r, :, 2 * C : 3 * C] = before.astype(BF)

    def window(dt, dy):
        return cot3[2 - dt : 4, 2 - dy : 4 - dy].reshape((dt + 2) * R * W, 3 * C)

    def act_grad_part(dt, dy, first):
        t0 = 9 * dt + 3 * dy
        taps = jnp.concatenate([kbuf[(t0 + d) * C : (t0 + d + 1) * C] for d in range(3)], axis=1)
        out = dot(taps, window(dt, dy), 1, 1)
        n = (dt + 2) * R * W
        if first:
            ag[...] = out
        else:
            ag[:, :n] += out

    load_cot.wait()
    build_cot((1, 2))

    for cp in lat_x:
        cp.wait_recv()
    for k in (3, 1, 2):
        src = latg.at[2 * ((x + k) % 4) + core]
        lat_s.append(send(src, src, sib))

    load_ker.wait()
    act_grad_part(2, 1, True)
    for cp in lat_s:
        cp.wait_recv()

    for f in range(F):
        slot = jnp.int32(0)
        for s in range(CLIPS * F):
            slot = jnp.where(route[s] == clip * F + f, s, slot)
        v = unpack(latg, slot) * live[f]
        lat4[f, 1] = v[:LAT].astype(BF)
        lat4[f, 2] = v[LAT:].astype(BF)
    lat_h = [send(lat4.at[:, 1], lat4.at[:, 3], tm), send(lat4.at[:, 2], lat4.at[:, 0], tp)]
    act_grad_part(1, 1, False)
    act_grad_part(0, 1, False)
    for cp in lat_h:
        cp.wait_recv()

    for f in range(F):
        for r in range(4):
            v = lat4[f, r].astype(F32) * edge[r]
            s3[f, r, 0:LAT] = pltpu.roll(v, 1, 1).astype(BF)
            s3[f, r, LAT : 2 * LAT] = v.astype(BF)
            s3[f, r, 2 * LAT :] = pltpu.roll(v, LANES - 1, 1).astype(BF)
    for f in range(F):
        for r in range(R):
            for dt in range(3):
                for dy in range(3):
                    at_rows = slice((3 * dt + dy) * 48, (3 * dt + dy + 1) * 48)
                    at_cols = slice((2 * f + r) * W, (2 * f + r + 1) * W)
                    if f - 2 + dt >= 0:
                        xt[at_rows, at_cols] = s3[f - 2 + dt, r + dy, :, 0:W]
                    else:
                        xt[at_rows, at_cols] = jnp.zeros((48, W), BF)
    gain = as_column(gain_in)
    hid[...] = dot(ink[...], xt[...], 0, 0) + as_column(bias_in)

    def norm_step(n, carry):
        cols = pl.ds(pl.multiple_of(n * 128, 128), 128)
        h = hid[:, cols]
        inv = lax.rsqrt(jnp.mean(h * h, axis=0, keepdims=True) + EPS)
        normed = h * inv * gain
        act[:, cols] = (normed * sigmoid(normed)).astype(BF)
        inv_ref[:, cols] = inv
        return carry

    lax.fori_loop(0, POS // 128, norm_step, 0)

    def late_rows():
        for cp in halo:
            cp.wait_recv()
        build_cot((0, 3))

    def weight_part(g, order):
        dt, dy = g // 3, g % 3
        out = dot(act[:, : (dt + 2) * R * W], window(dt, dy), 1, 0)
        for k in range(9):
            v = out[:, 128 * k : 128 * (k + 1)]
            if order == "yz":
                v = jnp.concatenate(
                    [v[24 * (4 * b + a) : 24 * (4 * b + a) + 24] for a in range(4) for b in range(4)], axis=0
                )
            gbuf[9 * g + k] = v.astype(BF)

    def pick(a, b):
        return jnp.where(core == 0, a, b)

    def wave_steps(ranges, order, off):
        total = sum(n for _, n in ranges)
        mine = pl.ds(off, total)
        if order == "zy":
            (a, ap, am), (b, bp, bm, bo) = (z, zp, zm), (y, yp, ym, yo)
        else:
            (a, ap, am), (b, bp, bm, bo) = (y, yp, ym), (z, zp, zm, zo)
        st = {}

        def rows_a(k):
            return 96 * ((a + k) % 4)

        def rows_b(k):
            to = (b + k) % 4
            return pl.multiple_of(48 * (to // 2) + 16 * (to % 2), 16)

        def s0():
            st["c"], at0 = [], off
            for first, n in ranges:
                mirror = 81 - first - n
                src = gbuf.at[pl.ds(pick(mirror, first), n)]
                st["c"].append(send(src, own.at[pl.ds(at0, n)], sib))
                at0 += n

        def s1():
            for cp in st["c"]:
                cp.wait_recv()
            at0 = off
            for first, n in ranges:
                start = pick(first, 81 - first - n)

                def body(k, carry, start=start, at0=at0):
                    own[at0 + k] = own[at0 + k] + gbuf[start + k]
                    return carry

                lax.fori_loop(0, n, body, 0)
                at0 += n
            r = pl.multiple_of(rows_a(2), 48)
            st["p1"] = send(own.at[mine, pl.ds(r, 48)], r1.at[mine, 0], ap)
            st["m1"] = send(own.at[mine, pl.ds(pl.multiple_of(r + 48, 48), 48)], r1.at[mine, 1], am)

        def s2():
            for side, k, shift, device in ((0, 1, 0, ap), (1, 3, 48, am)):
                st["pm"[side] + "1"].wait_recv()
                rows = pl.ds(pl.multiple_of(rows_a(k) + shift, 48), 48)

                def body(t, carry, rows=rows, side=side):
                    own[off + t, rows] = own[off + t, rows] + r1[off + t, side]
                    return carry

                lax.fori_loop(0, total, body, 0)
                st["pm"[side] + "2"] = send(
                    own.at[mine, pl.ds(pl.multiple_of(rows_a(k), 96), 96)], r2.at[mine, side], device
                )

        def s3_():
            st["p2"].wait_recv()
            st["m2"].wait_recv()
            rows = pl.ds(pl.multiple_of(rows_a(0), 96), 96)

            def body(t, carry):
                i = off + t
                res[i] = (own[i, rows].astype(F32) + r2[i, 0].astype(F32) + r2[i, 1].astype(F32)).astype(BF)
                return carry

            lax.fori_loop(0, total, body, 0)
            st["q"] = [
                send(res.at[mine, pl.ds(rows_b(k), 32)], q.at[mine, i], device)
                for i, (k, device) in enumerate(((1, bp), (3, bm), (2, bo)))
            ]

        def s4():
            for cp in st["q"]:
                cp.wait_recv()
            rows = pl.ds(rows_b(0), 32)
            odd = (b % 2) == 1
            at0 = off
            for first, n in ranges:
                mirror = 81 - first - n
                place = pick(
                    11 * (first // 20) + first % 20, 11 * ((mirror - 10) // 20) + (mirror - 10) % 20
                )

                def body(t, carry, place=place, at0=at0):
                    i = at0 + t
                    v = res[i, rows].astype(F32) + q[i, 0].astype(F32)
                    v += q[i, 1].astype(F32) + q[i, 2].astype(F32)
                    v = jnp.where(odd, v[8:], v[:24])
                    fin[place + t] = jnp.concatenate([v, jnp.zeros((8, 128), F32)], axis=0).astype(BF)
                    return carry

                lax.fori_loop(0, n, body, 0)
                at0 += n

        return [s0, s1, s2, s3_, s4]

    waves, off = [], 0
    for _, ranges, order in WAVES:
        waves.append(wave_steps(ranges, order, off))
        off += sum(n for _, n in ranges)
    orders = {g: order for groups, _, order in WAVES for g in groups}

    def x_sends():
        def win(k):
            return pl.ds(11 * ((x + k) % 4), 11)

        st["x"] = [send(fin.at[win(k)], xr.at[i], d) for i, (k, d) in enumerate(((1, xp), (3, xm), (2, xo)))]

    def hidden_grad():
        def grad_step(n, carry):
            cols = pl.ds(pl.multiple_of(n * 128, 128), 128)
            h, inv = hid[:, cols], inv_ref[:, cols]
            normed = h * inv * gain
            s = sigmoid(normed)
            gained = ag[:, cols] * s * (1.0 + normed * (1.0 - s)) * gain
            inner = jnp.mean(gained * h, axis=0, keepdims=True)
            hg[:, cols] = (inv * gained - h * (inv * inv * inv * inner)).astype(BF)
            return carry

        lax.fori_loop(0, POS // 128, grad_step, 0)
        yt[...] = dot(ink[...], hg[...], 1, 0)

        col = lax.broadcasted_iota(jnp.int32, (LAT, POS), 1) % W
        summed = []
        for g in range(9):
            base = 48 * g
            after = jnp.where(col == W - 1, 0.0, pltpu.roll(yt[base : base + LAT], POS - 1, 1))
            before = jnp.where(col == 0, 0.0, pltpu.roll(yt[base + 2 * LAT : base + 3 * LAT], 1, 1))
            summed.append(yt[base + LAT : base + 2 * LAT] + after + before)
        for f in range(F):
            for r in range(4):
                total = None
                for dt in range(3):
                    for dy in range(3):
                        fh, rh = f + 2 - dt, r - dy
                        if fh < F and 0 <= rh < R:
                            p = (2 * fh + rh) * W
                            term = summed[3 * dt + dy][:, p : p + W]
                            total = term if total is None else total + term
                lg[f, r, :, 0:W] = total
                lg[f, r, :, W:] = jnp.zeros((LAT, LANES - W), F32)
        st["lg"] = [send(lg.at[:, 0], lgr.at[:, 1], tm), send(lg.at[:, 3], lgr.at[:, 0], tp)]

    def clip_grad():
        for cp in st["lg"]:
            cp.wait_recv()
        tiles = []
        for f in range(F):
            first = (lg[f, 1] + lgr[f, 0] * top) * live[f]
            second = (lg[f, 2] + lgr[f, 1] * bottom) * live[f]
            tiles.append(jnp.concatenate([first, second], axis=0))
        pack(tiles, latg2.at[clip])
        st["bx"] = [send(latg2.at[clip], latg2.at[clip], d) for d in (xp, xm, xo)]
        st["bs"] = [send(latg2.at[clip], latg2.at[clip], sib)]

    def pass_on():
        for cp in st["bx"]:
            cp.wait_recv()
        for k in (3, 1, 2):
            src = latg2.at[2 * ((x + k) % 4) + core]
            st["bs"].append(send(src, src, sib))

    def latent_grad():
        for cp in st["bs"]:
            cp.wait_recv()
        tiles = [unpack(latg2, route[clip * F + j]) for j in range(F)]
        tr2[...] = jnp.concatenate(tiles, axis=0).T
        for jr in range(8):
            u = jnp.zeros((20, 128), F32)
            for q8 in range(8):
                u = jnp.where(lane16 == q8, roll(tr2[pl.ds(q8, 20, stride=8), :], LAT * (q8 - jr)), u)
            tr1[jr * 24 : jr * 24 + 20] = u
        flat = jnp.concatenate([tr1[pl.ds(g, 8, stride=24), :] for g in range(20)], axis=1)
        for j in range(F):
            out_lat[j] = flat[R * j : R * j + R].astype(BF)

    st = {}
    tail = {"halo": late_rows, "hidden": hidden_grad, "clip": clip_grad, "pass": pass_on, "out": latent_grad, "x": x_sends}
    for kind, k in SCHEDULE:
        if kind == "G":
            weight_part(k, orders[k])
        elif kind == "A":
            act_grad_part(k // 3, k % 3, False)
        elif kind == "T":
            tail[k]()
        else:
            waves[kind][k]()

    for cp in st["x"]:
        cp.wait_recv()
    v = fin[pl.ds(11 * x, 11)].astype(F32) + xr[0].astype(F32)
    v += xr[1].astype(F32) + xr[2].astype(F32)
    v = v[:, :24] * (1.0 / math.sqrt(CLIPS * F * H * W))
    flat = jnp.concatenate([v[k] for k in range(11)], axis=1)
    out_wg[...] = pltpu.roll(flat, 11 * 128 - 16 * clip, 1)[:, :1296]

    for cp in copies:
        cp.wait_send()


def on_device(latents, tile_route, lengths, reward_grad, in_kernel, in_bias, norm_gain, kernel_):
    vmem = pl.BlockSpec(memory_space=pltpu.VMEM)
    smem = pl.BlockSpec(memory_space=pltpu.SMEM)
    hbm = pl.BlockSpec(memory_space=pl.ANY)

    def v(*shape, dtype=BF):
        return pltpu.VMEM(shape, dtype)

    return pl.pallas_call(
        kernel,
        out_shape=(
            jax.ShapeDtypeStruct((F, R, W * LAT), BF),
            jax.ShapeDtypeStruct((24, 1296), F32),
        ),
        in_specs=[smem, smem, vmem, hbm, vmem, vmem, vmem, hbm],
        out_specs=(vmem, vmem),
        scratch_shapes=[
            v(F, 4, W, C),
            v(F, 4, W, 3 * C),
            v(27 * C, C),
            v(192, 128, dtype=F32),
            v(LANES, 128, dtype=F32),
            v(F + 1, R * LAT, 128),
            v(CLIPS, F + 1, R * LAT, 128),
            v(F, 4, LAT, LANES),
            v(F, 4, 3 * LAT, LANES),
            v(27 * LAT, POS),
            v(C, POS, dtype=F32),
            v(C, POS),
            v(1, POS, dtype=F32),
            v(C, POS, dtype=F32),
            v(C, POS),
            v(27 * LAT, POS, dtype=F32),
            v(F, 4, LAT, LANES, dtype=F32),
            v(F, 2, LAT, LANES, dtype=F32),
            v(CLIPS, F + 1, R * LAT, 128),
            v(81, C, 128),
            v(OWN, C, 128),
            v(OWN, 2, 48, 128),
            v(OWN, 2, 96, 128),
            v(OWN, 96, 128),
            v(OWN, 3, 32, 128),
            v(OWN, 32, 128),
            v(3, 11, 32, 128),
            pltpu.SemaphoreType.DMA((2,)),
            pltpu.SemaphoreType.DMA((96,)),
            pltpu.SemaphoreType.DMA((96,)),
        ],
        compiler_params=pltpu.CompilerParams(
            collective_id=0, has_side_effects=True, vmem_limit_bytes=62 * 2**20
        ),
        name="backward",
    )(
        tile_route, lengths, latents, reward_grad, in_kernel, in_bias, norm_gain, kernel_,
    )


def solution(mesh):
    return jax.shard_map(
        on_device,
        mesh=mesh,
        in_specs=(
            P("clip", "tile", None),
            P(),
            P(),
            P("clip", None, "tile", None, None),
            P(),
            P(),
            P(),
            P(),
        ),
        out_specs=(P("clip", "tile", None), P("tile", "clip")),
        check_vma=False,
    )
```

time: 103 us -> 78.5 us (0.76)
  Pallas kernels: 93.3 us -> 74.6 us
  local copies, waits for them, and re-layouts: 8.41 us -> 3 us
    pallas_call x1, Pallas kernels: 93.3 us -> 74.6 us  [on_device(): pl.pallas_call(kernel, out_shape=(jax.ShapeDtypeStruct((F, R, W * LAT), B...]
    reshape x5 -> x0, local copies, waits for them, and re-layouts: 6.01 us -> none  [the longest x2 2.02 us: on_device(): lat_grad[:, :, :W].reshape(F, R, LAT, W).transpose(0, 1, 3, 2)]
    unnamed x1 -> x2, local copies, waits for them, and re-layouts: 1.57 us -> 3 us
where the time goes in v2:
time: 78.5 us; the launch traced here: 78.3 us
  Pallas kernels  74.6 us (95%)
  local copies, waits for them, and re-layouts  3 us (4%)
    pallas_call x1, Pallas kernels, on_device(): pl.pallas_call(kernel, out_shape=(jax.ShapeDtypeStruct((F, R, W * LAT), B...  74.6 us
    unnamed x2, local copies, waits for them, and re-layouts  3 us

profile of v2, /device:TPU:0, one launch (start us, length us, event | category | flops | bytes accessed | tf_op | source)
XLA Modules:
  0.0 78.3 jit_solution(3218095153376150562)
XLA Ops:
  0.6 74.6 %backward.1 = (bf16[4,2,2560]{2,1,0:T(2,128)(2,1)}, f32[24,1296]{1,0:T(8,128)}) custom-call(s32[32]{0:T(128)} %route.1, s32[8]{0:T(128)} %lengths.1, bf16[4,2,2560]{2,1,0:T(2,128)(2,1)} %lat_in.1, bf16[1,4,2,160,384]{4,3,2,1,0:T(8,128)(2,1)} %cot_in.1, bf16[432,384]{1,0:T(8,128)(2,1)} %ink.1, f32[384]{0:T(512)} %bias_in.1, f32[384]{0:T(512)} %gain_in.1, ...), custom_call_target="tpu_custom_call" | custom-call | tf_op jit(solution)/shard_map/backward/pallas_call | solution.py:450
  75.3 1.4 %copy.12 = bf16[4,2,2560]{2,1,0:T(2,128)(2,1)} copy(bf16[4,2,2560]{2,1,0:T(2,128)(2,1)} %get-tuple-element.4) | data formatting | bytes 81920
  76.7 1.6 %copy.13 = f32[24,1296]{1,0:T(8,128)} copy(f32[24,1296]{1,0:T(8,128)} %get-tuple-element.5) | data formatting | bytes 248832

commit v3 on v2

--- a/solution.py
+++ b/solution.py
@@ -15,20 +15,19 @@
 BF, F32 = jnp.bfloat16, jnp.float32
 
 WAVES = (
-    ((1, 7), ((9, 2), (63, 8)), "zy"),
-    ((4,), ((40, 5),), "zy"),
-    ((0, 8), ((0, 9),), "yz"),
+    ((1, 7), ((9, 2), (63, 8)), "yz"),
+    ((4,), ((40, 5),), "yz"),
+    ((0, 8), ((0, 9),), "zy"),
     ((2, 6), ((20, 7), (60, 3)), "zy"),
     ((3, 5), ((27, 4), (45, 6)), "yz"),
 )
 OWN = 44
 
 SCHEDULE = (
-    ("G", 1), ("G", 7), (0, 0), ("T", "halo"), ("G", 3), ("G", 5), (4, 0), (0, 1), ("G", 0), ("G", 8), (2, 0),
-    ("G", 4), (1, 0), (4, 1), ("G", 2), (0, 2), ("G", 6), (3, 0), (2, 1), (1, 1), ("A", 6), (4, 2), ("A", 3),
-    (3, 1), ("A", 0), (2, 2), (0, 3), ("A", 8), (1, 2), ("A", 5), ("A", 2), (3, 2), (4, 3), ("T", "hidden"),
-    (1, 3), (2, 3), (3, 3), (0, 4), ("T", "clip"), (1, 4), (4, 4), ("T", "pass"), (3, 4), (2, 4), ("T", "x"),
-    ("T", "out"),
+    ("G", 4), (1, 0), ("T", "late1"), ("T", "late0"), ("G", 6), (1, 1), ("G", 7), ("G", 5), ("G", 1), (0, 0),
+    (1, 2), ("G", 2), (3, 0), ("G", 3), (4, 0), ("G", 0), ("G", 8), (2, 0), (1, 3), (0, 1), (3, 1), (4, 1),
+    ("A", 6), (2, 1), (1, 4), ("A", 5), (0, 2), ("A", 3), (3, 2), ("A", 8), (4, 2), (2, 2), ("T", "hidden"),
+    (0, 3), (3, 3), (4, 3), (2, 3), ("T", "clip"), (0, 4), (3, 4), (2, 4), (4, 4), ("T", "x"), ("T", "out"),
 )
 
 
@@ -45,12 +44,12 @@
 
 
 def pack(tiles, ref):
-    rest = None
+    rest, dtype = None, ref.dtype
     for f in range(F):
-        ref[f] = tiles[f][:, :128].astype(BF)
+        ref[f] = tiles[f][:, :128].astype(dtype)
         part = roll(tiles[f][:, 128:], 32 * f)
         rest = part if rest is None else rest + part
-    ref[F] = rest.astype(BF)
+    ref[F] = rest.astype(dtype)
 
 
 def unpack(ref, slot):
@@ -70,7 +69,7 @@
 def kernel(
     route, lengths, lat_in, cot_in, ink, bias_in, gain_in, ker_in,
     out_lat, out_wg,
-    cotbuf, cot3, kbuf, tr1, tr2, stage, latg, lat4, s3, xt, hid, act, inv_ref, ag, hg, yt, lg, lgr, latg2,
+    cotbuf, cot3, kbuf, tr1, tr2, stage, latg, lat4, s3, xt, hid, act, inv_ref, ag, hg, yt, lg, lgs, lgr, latg2,
     gbuf, own, r1, r2, res, q, fin, xr,
     local_sem, send_sem, recv_sem,
 ):
@@ -85,10 +84,12 @@
 
     sib = at(clip=2 * x + 1 - core)
     xp, xm, xo = (at(clip=2 * ((x + k) % 4) + core) for k in (1, 3, 2))
+    others = tuple(at(clip=2 * ((x + k) % 4) + 1 - core) for k in (1, 3, 2))
+    group = (xp, xm, xo) + others + (sib,)
     zp, zm, zo = (at(tile=4 * ((z + k) % 4) + y) for k in (1, 3, 2))
     yp, ym, yo = (at(tile=4 * z + (y + k) % 4) for k in (1, 3, 2))
     tp, tm = (at(tile=(tile + k) % 16) for k in (1, 15))
-    peers = (sib, xp, xm, xo, zp, zm, zo, yp, ym, yo, tp, tm)
+    peers = (sib, xp, xm, xo, zp, zm, zo, yp, ym, yo, tp, tm) + others
 
     copies = []
 
@@ -125,11 +126,14 @@
 
     pl.semaphore_wait(barrier, len(peers))
 
-    lat_x = [send(stage, latg.at[clip], d) for d in (xp, xm, xo)]
-    lat_s = [send(stage, latg.at[clip], sib)]
+    lat_g = [send(stage, latg.at[clip], d) for d in group]
+    parts = (slice(2, 4), slice(1, 2), slice(0, 1))
     halo = [
-        send(cot_in.at[0, :, 0], cotbuf.at[:, 3], tm),
-        send(cot_in.at[0, :, 1], cotbuf.at[:, 0], tp),
+        [
+            send(cot_in.at[0, part, 0], cotbuf.at[part, 3], tm),
+            send(cot_in.at[0, part, 1], cotbuf.at[part, 0], tp),
+        ]
+        for part in parts
     ]
     latg[clip] = stage[...]
 
@@ -139,9 +143,9 @@
     bottom = jnp.where(tile < 15, 1.0, 0.0).astype(F32)
     edge = (top, 1.0, 1.0, bottom)
 
-    def build_cot(rows):
+    def build_cot(rows, frames):
         col = lax.broadcasted_iota(jnp.int32, (W, C), 0)
-        for f in range(F):
+        for f in frames:
             for r in rows:
                 v = cotbuf[f, r].astype(F32) * (live[f] * edge[r])
                 after = jnp.where(col == W - 1, 0.0, pltpu.roll(v, W - 1, 0))
@@ -163,18 +167,19 @@
         else:
             ag[:, :n] += out
 
+    def late_rows(k):
+        for cp in halo[k]:
+            cp.wait_recv()
+        build_cot((0, 3), range(F)[parts[k]])
+
     load_cot.wait()
-    build_cot((1, 2))
-
-    for cp in lat_x:
-        cp.wait_recv()
-    for k in (3, 1, 2):
-        src = latg.at[2 * ((x + k) % 4) + core]
-        lat_s.append(send(src, src, sib))
+    build_cot((1, 2), range(F))
 
     load_ker.wait()
     act_grad_part(2, 1, True)
-    for cp in lat_s:
+    act_grad_part(1, 1, False)
+    act_grad_part(0, 1, False)
+    for cp in lat_g:
         cp.wait_recv()
 
     for f in range(F):
@@ -185,8 +190,9 @@
         lat4[f, 1] = v[:LAT].astype(BF)
         lat4[f, 2] = v[LAT:].astype(BF)
     lat_h = [send(lat4.at[:, 1], lat4.at[:, 3], tm), send(lat4.at[:, 2], lat4.at[:, 0], tp)]
-    act_grad_part(1, 1, False)
-    act_grad_part(0, 1, False)
+    late_rows(0)
+    act_grad_part(0, 0, False)
+    act_grad_part(0, 2, False)
     for cp in lat_h:
         cp.wait_recv()
 
@@ -220,11 +226,6 @@
 
     lax.fori_loop(0, POS // 128, norm_step, 0)
 
-    def late_rows():
-        for cp in halo:
-            cp.wait_recv()
-        build_cot((0, 3))
-
     def weight_part(g, order):
         dt, dy = g // 3, g % 3
         out = dot(act[:, : (dt + 2) * R * W], window(dt, dy), 1, 0)
@@ -274,7 +275,7 @@
                     own[at0 + k] = own[at0 + k] + gbuf[start + k]
                     return carry
 
-                lax.fori_loop(0, n, body, 0)
+                lax.fori_loop(0, n, body, 0, unroll=True)
                 at0 += n
             r = pl.multiple_of(rows_a(2), 48)
             st["p1"] = send(own.at[mine, pl.ds(r, 48)], r1.at[mine, 0], ap)
@@ -289,7 +290,7 @@
                     own[off + t, rows] = own[off + t, rows] + r1[off + t, side]
                     return carry
 
-                lax.fori_loop(0, total, body, 0)
+                lax.fori_loop(0, total, body, 0, unroll=True)
                 st["pm"[side] + "2"] = send(
                     own.at[mine, pl.ds(pl.multiple_of(rows_a(k), 96), 96)], r2.at[mine, side], device
                 )
@@ -304,7 +305,7 @@
                 res[i] = (own[i, rows].astype(F32) + r2[i, 0].astype(F32) + r2[i, 1].astype(F32)).astype(BF)
                 return carry
 
-            lax.fori_loop(0, total, body, 0)
+            lax.fori_loop(0, total, body, 0, unroll=True)
             st["q"] = [
                 send(res.at[mine, pl.ds(rows_b(k), 32)], q.at[mine, i], device)
                 for i, (k, device) in enumerate(((1, bp), (3, bm), (2, bo)))
@@ -330,7 +331,7 @@
                     fin[place + t] = jnp.concatenate([v, jnp.zeros((8, 128), F32)], axis=0).astype(BF)
                     return carry
 
-                lax.fori_loop(0, n, body, 0)
+                lax.fori_loop(0, n, body, 0, unroll=True)
                 at0 += n
 
         return [s0, s1, s2, s3_, s4]
@@ -380,29 +381,30 @@
                             total = term if total is None else total + term
                 lg[f, r, :, 0:W] = total
                 lg[f, r, :, W:] = jnp.zeros((LAT, LANES - W), F32)
-        st["lg"] = [send(lg.at[:, 0], lgr.at[:, 1], tm), send(lg.at[:, 3], lgr.at[:, 0], tp)]
+        pack([lg[f, 0] for f in range(F)], lgs.at[0])
+        pack([lg[f, 3] for f in range(F)], lgs.at[1])
+        st["lg"] = [send(lgs.at[0], lgr.at[1], tm), send(lgs.at[1], lgr.at[0], tp)]
 
     def clip_grad():
         for cp in st["lg"]:
             cp.wait_recv()
         tiles = []
+        narrow = lax.broadcasted_iota(jnp.int32, (LAT, 128), 1) < 32
         for f in range(F):
-            first = (lg[f, 1] + lgr[f, 0] * top) * live[f]
-            second = (lg[f, 2] + lgr[f, 1] * bottom) * live[f]
+            from_up, from_down = (
+                jnp.concatenate(
+                    [lgr[k, f], jnp.where(narrow, roll(lgr[k, F], -32 * f), 0.0)], axis=1
+                )
+                for k in range(2)
+            )
+            first = (lg[f, 1] + from_up * top) * live[f]
+            second = (lg[f, 2] + from_down * bottom) * live[f]
             tiles.append(jnp.concatenate([first, second], axis=0))
         pack(tiles, latg2.at[clip])
-        st["bx"] = [send(latg2.at[clip], latg2.at[clip], d) for d in (xp, xm, xo)]
-        st["bs"] = [send(latg2.at[clip], latg2.at[clip], sib)]
-
-    def pass_on():
-        for cp in st["bx"]:
-            cp.wait_recv()
-        for k in (3, 1, 2):
-            src = latg2.at[2 * ((x + k) % 4) + core]
-            st["bs"].append(send(src, src, sib))
+        st["back"] = [send(latg2.at[clip], latg2.at[clip], d) for d in group]
 
     def latent_grad():
-        for cp in st["bs"]:
+        for cp in st["back"]:
             cp.wait_recv()
         tiles = [unpack(latg2, route[clip * F + j]) for j in range(F)]
         tr2[...] = jnp.concatenate(tiles, axis=0).T
@@ -416,7 +418,7 @@
             out_lat[j] = flat[R * j : R * j + R].astype(BF)
 
     st = {}
-    tail = {"halo": late_rows, "hidden": hidden_grad, "clip": clip_grad, "pass": pass_on, "out": latent_grad, "x": x_sends}
+    tail = {"late1": lambda: late_rows(1), "late0": lambda: late_rows(2), "hidden": hidden_grad, "clip": clip_grad, "out": latent_grad, "x": x_sends}
     for kind, k in SCHEDULE:
         if kind == "G":
             weight_part(k, orders[k])
@@ -473,7 +475,8 @@
             v(C, POS),
             v(27 * LAT, POS, dtype=F32),
             v(F, 4, LAT, LANES, dtype=F32),
-            v(F, 2, LAT, LANES, dtype=F32),
+            v(2, F + 1, LAT, 128, dtype=F32),
+            v(2, F + 1, LAT, 128, dtype=F32),
             v(CLIPS, F + 1, R * LAT, 128),
             v(81, C, 128),
             v(OWN, C, 128),

time: 78.5 us -> 76 us (0.968)
  Pallas kernels: 74.6 us -> 72.2 us
    pallas_call x1, Pallas kernels: 74.6 us -> 72.2 us  [on_device(): pl.pallas_call(kernel, out_shape=(jax.ShapeDtypeStruct((F, R, W * LAT), B...]
where the time goes in v3:
time: 76 us; the launch traced here: 75.8 us
  Pallas kernels  72.2 us (95%)
  local copies, waits for them, and re-layouts  3 us (4%)
    pallas_call x1, Pallas kernels, on_device(): pl.pallas_call(kernel, out_shape=(jax.ShapeDtypeStruct((F, R, W * LAT), B...  72.2 us
    unnamed x2, local copies, waits for them, and re-layouts  3 us

profile of v3, /device:TPU:0, one launch (start us, length us, event | category | flops | bytes accessed | tf_op | source)
XLA Modules:
  0.0 75.8 jit_solution(11452212426552981683)
XLA Ops:
  0.6 72.2 %backward.1 = (bf16[4,2,2560]{2,1,0:T(2,128)(2,1)}, f32[24,1296]{1,0:T(8,128)}) custom-call(s32[32]{0:T(128)} %route.1, s32[8]{0:T(128)} %lengths.1, bf16[4,2,2560]{2,1,0:T(2,128)(2,1)} %lat_in.1, bf16[1,4,2,160,384]{4,3,2,1,0:T(8,128)(2,1)} %cot_in.1, bf16[432,384]{1,0:T(8,128)(2,1)} %ink.1, f32[384]{0:T(512)} %bias_in.1, f32[384]{0:T(512)} %gain_in.1, ...), custom_call_target="tpu_custom_call" | custom-call | tf_op jit(solution)/shard_map/backward/pallas_call | solution.py:452
  72.8 1.4 %copy.12 = bf16[4,2,2560]{2,1,0:T(2,128)(2,1)} copy(bf16[4,2,2560]{2,1,0:T(2,128)(2,1)} %get-tuple-element.4) | data formatting | bytes 81920
  74.2 1.6 %copy.13 = f32[24,1296]{1,0:T(8,128)} copy(f32[24,1296]{1,0:T(8,128)} %get-tuple-element.5) | data formatting | bytes 248832

commit v4 on v3

--- a/solution.py
+++ b/solution.py
@@ -22,12 +22,15 @@
     ((3, 5), ((27, 4), (45, 6)), "yz"),
 )
 OWN = 44
+FIXED = 96
+PAIRS = sum((n + 1) // 2 for _, ranges, _ in WAVES for _, n in ranges)
 
 SCHEDULE = (
-    ("G", 4), (1, 0), ("T", "late1"), ("T", "late0"), ("G", 6), (1, 1), ("G", 7), ("G", 5), ("G", 1), (0, 0),
-    (1, 2), ("G", 2), (3, 0), ("G", 3), (4, 0), ("G", 0), ("G", 8), (2, 0), (1, 3), (0, 1), (3, 1), (4, 1),
-    ("A", 6), (2, 1), (1, 4), ("A", 5), (0, 2), ("A", 3), (3, 2), ("A", 8), (4, 2), (2, 2), ("T", "hidden"),
-    (0, 3), (3, 3), (4, 3), (2, 3), ("T", "clip"), (0, 4), (3, 4), (2, 4), (4, 4), ("T", "x"), ("T", "out"),
+    ("G", 7), ("G", 1), (0, 0), ("G", 2), ("T", "late1"), ("T", "late0"), ("G", 6), (3, 0), (0, 1), ("G", 5),
+    ("G", 3), (4, 0), ("G", 8), (3, 1), (0, 2), ("G", 0), (2, 0), (4, 1), ("G", 4), (1, 0), ("A", 5), (2, 1),
+    (3, 2), ("A", 3), (1, 1), ("A", 6), (0, 3), ("A", 8), (2, 2), (4, 2), ("T", "hidden"), (1, 2), (3, 3),
+    (0, 4), (4, 3), ("T", "clip"), (0, 5), (1, 3), (2, 3), (3, 4), (4, 4), (1, 4), (2, 4), ("T", "out"),
+    (3, 5), (4, 5), (1, 5), (2, 5),
 )
 
 
@@ -70,7 +73,7 @@
     route, lengths, lat_in, cot_in, ink, bias_in, gain_in, ker_in,
     out_lat, out_wg,
     cotbuf, cot3, kbuf, tr1, tr2, stage, latg, lat4, s3, xt, hid, act, inv_ref, ag, hg, yt, lg, lgs, lgr, latg2,
-    gbuf, own, r1, r2, res, q, fin, xr,
+    gbuf, own, r1, r2, sb, q, fin, fr, outf,
     local_sem, send_sem, recv_sem,
 ):
     clip, tile = lax.axis_index("clip"), lax.axis_index("tile")
@@ -95,6 +98,7 @@
 
     def send(src, dst, device):
         n = len(copies)
+        assert n < FIXED
         cp = pltpu.make_async_remote_copy(
             src_ref=src, dst_ref=dst, send_sem=send_sem.at[n], recv_sem=recv_sem.at[n],
             device_id=device, device_id_type=MESH,
@@ -240,7 +244,9 @@
     def pick(a, b):
         return jnp.where(core == 0, a, b)
 
-    def wave_steps(ranges, order, off):
+    to_owner = []
+
+    def wave_steps(ranges, order, off, poff):
         total = sum(n for _, n in ranges)
         mine = pl.ds(off, total)
         if order == "zy":
@@ -252,10 +258,6 @@
         def rows_a(k):
             return 96 * ((a + k) % 4)
 
-        def rows_b(k):
-            to = (b + k) % 4
-            return pl.multiple_of(48 * (to // 2) + 16 * (to % 2), 16)
-
         def s0():
             st["c"], at0 = [], off
             for first, n in ranges:
@@ -300,53 +302,76 @@
             st["m2"].wait_recv()
             rows = pl.ds(pl.multiple_of(rows_a(0), 96), 96)
 
-            def body(t, carry):
-                i = off + t
-                res[i] = (own[i, rows].astype(F32) + r2[i, 0].astype(F32) + r2[i, 1].astype(F32)).astype(BF)
-                return carry
-
-            lax.fori_loop(0, total, body, 0, unroll=True)
+            def block(i):
+                return own[i, rows].astype(F32) + r2[i, 0].astype(F32) + r2[i, 1].astype(F32)
+
+            at0, p = off, poff
+            for _, n in ranges:
+                for i in range(at0, at0 + n, 2):
+                    one = block(i)
+                    two = block(i + 1) if i + 1 < at0 + n else jnp.zeros_like(one)
+                    for to in range(4):
+                        part = slice(24 * to, 24 * to + 24)
+                        sb[to, p] = jnp.concatenate([one[part], two[part]], axis=0).astype(BF)
+                    p += 1
+                at0 += n
+            pairs = pl.ds(poff, p - poff)
             st["q"] = [
-                send(res.at[mine, pl.ds(rows_b(k), 32)], q.at[mine, i], device)
+                send(sb.at[(b + k) % 4, pairs], q.at[i, pairs], device)
                 for i, (k, device) in enumerate(((1, bp), (3, bm), (2, bo)))
             ]
 
         def s4():
             for cp in st["q"]:
                 cp.wait_recv()
-            rows = pl.ds(rows_b(0), 32)
-            odd = (b % 2) == 1
-            at0 = off
+            p, st["owner"] = poff, []
             for first, n in ranges:
+                count = (n + 1) // 2
+                for i in range(p, p + count):
+                    v = sb[b, i].astype(F32) + q[0, i].astype(F32)
+                    fin[i] = (v + q[1, i].astype(F32) + q[2, i].astype(F32)).astype(BF)
                 mirror = 81 - first - n
-                place = pick(
-                    11 * (first // 20) + first % 20, 11 * ((mirror - 10) // 20) + (mirror - 10) % 20
+                owner = pick(first // 20, (mirror - 10) // 20)
+                base = FIXED + 4 * len(to_owner)
+                cp = pltpu.make_async_remote_copy(
+                    src_ref=fin.at[pl.ds(p, count)], dst_ref=fr.at[x, pl.ds(p, count)],
+                    send_sem=send_sem.at[base], recv_sem=recv_sem.at[base + x],
+                    device_id=at(clip=2 * owner + core), device_id_type=MESH,
                 )
-
-                def body(t, carry, place=place, at0=at0):
-                    i = at0 + t
-                    v = res[i, rows].astype(F32) + q[i, 0].astype(F32)
-                    v += q[i, 1].astype(F32) + q[i, 2].astype(F32)
-                    v = jnp.where(odd, v[8:], v[:24])
-                    fin[place + t] = jnp.concatenate([v, jnp.zeros((8, 128), F32)], axis=0).astype(BF)
-                    return carry
-
-                lax.fori_loop(0, n, body, 0, unroll=True)
-                at0 += n
-
-        return [s0, s1, s2, s3_, s4]
-
-    waves, off = [], 0
+                to_owner.append((owner, cp))
+                st["owner"].append((owner, base, p, n, pick(first % 20, (mirror - 10) % 20)))
+                pl.when(owner != x)(cp.start)
+                p += count
+
+        def s5():
+            for owner, base, p, n, place in st["owner"]:
+
+                @pl.when(owner == x)
+                def _(base=base, p=p, n=n, place=place):
+                    count = (n + 1) // 2
+                    others_x = [(x + k) % 4 for k in (1, 3, 2)]
+                    for k in others_x:
+                        pltpu.make_async_remote_copy(
+                            src_ref=fin.at[pl.ds(p, count)], dst_ref=fr.at[k, pl.ds(p, count)],
+                            send_sem=send_sem.at[base], recv_sem=recv_sem.at[base + k],
+                            device_id=xp, device_id_type=MESH,
+                        ).wait_recv()
+                    for i in range(count):
+                        v = fin[p + i].astype(F32)
+                        for k in others_x:
+                            v += fr[k, p + i].astype(F32)
+                        outf[place + 2 * i] = v[:24]
+                        if 2 * i + 1 < n:
+                            outf[place + 2 * i + 1] = v[24:]
+
+        return [s0, s1, s2, s3_, s4, s5]
+
+    waves, off, poff = [], 0, 0
     for _, ranges, order in WAVES:
-        waves.append(wave_steps(ranges, order, off))
+        waves.append(wave_steps(ranges, order, off, poff))
         off += sum(n for _, n in ranges)
+        poff += sum((n + 1) // 2 for _, n in ranges)
     orders = {g: order for groups, _, order in WAVES for g in groups}
-
-    def x_sends():
-        def win(k):
-            return pl.ds(11 * ((x + k) % 4), 11)
-
-        st["x"] = [send(fin.at[win(k)], xr.at[i], d) for i, (k, d) in enumerate(((1, xp), (3, xm), (2, xo)))]
 
     def hidden_grad():
         def grad_step(n, carry):
@@ -418,7 +443,7 @@
             out_lat[j] = flat[R * j : R * j + R].astype(BF)
 
     st = {}
-    tail = {"late1": lambda: late_rows(1), "late0": lambda: late_rows(2), "hidden": hidden_grad, "clip": clip_grad, "out": latent_grad, "x": x_sends}
+    tail = {"late1": lambda: late_rows(1), "late0": lambda: late_rows(2), "hidden": hidden_grad, "clip": clip_grad, "out": latent_grad}
     for kind, k in SCHEDULE:
         if kind == "G":
             weight_part(k, orders[k])
@@ -429,16 +454,14 @@
         else:
             waves[kind][k]()
 
-    for cp in st["x"]:
-        cp.wait_recv()
-    v = fin[pl.ds(11 * x, 11)].astype(F32) + xr[0].astype(F32)
-    v += xr[1].astype(F32) + xr[2].astype(F32)
-    v = v[:, :24] * (1.0 / math.sqrt(CLIPS * F * H * W))
-    flat = jnp.concatenate([v[k] for k in range(11)], axis=1)
+    scale = 1.0 / math.sqrt(CLIPS * F * H * W)
+    flat = jnp.concatenate([outf[k] * scale for k in range(11)], axis=1)
     out_wg[...] = pltpu.roll(flat, 11 * 128 - 16 * clip, 1)[:, :1296]
 
     for cp in copies:
         cp.wait_send()
+    for owner, cp in to_owner:
+        pl.when(owner != x)(cp.wait_send)
 
 
 def on_device(latents, tile_route, lengths, reward_grad, in_kernel, in_bias, norm_gain, kernel_):
@@ -482,13 +505,14 @@
             v(OWN, C, 128),
             v(OWN, 2, 48, 128),
             v(OWN, 2, 96, 128),
-            v(OWN, 96, 128),
-            v(OWN, 3, 32, 128),
-            v(OWN, 32, 128),
-            v(3, 11, 32, 128),
+            v(4, PAIRS, 48, 128),
+            v(3, PAIRS, 48, 128),
+            v(PAIRS, 48, 128),
+            v(4, PAIRS, 48, 128),
+            v(11, 24, 128, dtype=F32),
             pltpu.SemaphoreType.DMA((2,)),
-            pltpu.SemaphoreType.DMA((96,)),
-            pltpu.SemaphoreType.DMA((96,)),
+            pltpu.SemaphoreType.DMA((FIXED + 36,)),
+            pltpu.SemaphoreType.DMA((FIXED + 36,)),
         ],
         compiler_params=pltpu.CompilerParams(
             collective_id=0, has_side_effects=True, vmem_limit_bytes=62 * 2**20

time: 76 us -> 76.2 us (level)
  no operation moved by 1% of the time
where the time goes in v4:
time: 76.2 us; the launch traced here: 76 us
  Pallas kernels  72.4 us (95%)
  local copies, waits for them, and re-layouts  3 us (4%)
    pallas_call x1, Pallas kernels, on_device(): pl.pallas_call(kernel, out_shape=(jax.ShapeDtypeStruct((F, R, W * LAT), B...  72.4 us
    unnamed x2, local copies, waits for them, and re-layouts  3 us

profile of v4, /device:TPU:0, one launch (start us, length us, event | category | flops | bytes accessed | tf_op | source)
XLA Modules:
  0.0 76.0 jit_solution(3958130451510286769)
XLA Ops:
  0.6 72.4 %backward.1 = (bf16[4,2,2560]{2,1,0:T(2,128)(2,1)}, f32[24,1296]{1,0:T(8,128)}) custom-call(s32[32]{0:T(128)} %route.1, s32[8]{0:T(128)} %lengths.1, bf16[4,2,2560]{2,1,0:T(2,128)(2,1)} %lat_in.1, bf16[1,4,2,160,384]{4,3,2,1,0:T(8,128)(2,1)} %cot_in.1, bf16[432,384]{1,0:T(8,128)(2,1)} %ink.1, f32[384]{0:T(512)} %bias_in.1, f32[384]{0:T(512)} %gain_in.1, ...), custom_call_target="tpu_custom_call" | custom-call | tf_op jit(solution)/shard_map/backward/pallas_call | solution.py:475
  73.0 1.4 %copy.12 = bf16[4,2,2560]{2,1,0:T(2,128)(2,1)} copy(bf16[4,2,2560]{2,1,0:T(2,128)(2,1)} %get-tuple-element.4) | data formatting | bytes 81920
  74.4 1.6 %copy.13 = f32[24,1296]{1,0:T(8,128)} copy(f32[24,1296]{1,0:T(8,128)} %get-tuple-element.5) | data formatting | bytes 248832

commit v5 on v4

--- a/solution.py
+++ b/solution.py
@@ -15,22 +15,21 @@
 BF, F32 = jnp.bfloat16, jnp.float32
 
 WAVES = (
-    ((1, 7), ((9, 2), (63, 8)), "yz"),
+    ((1, 7), ((9, 2), (63, 8)), "zy"),
     ((4,), ((40, 5),), "yz"),
     ((0, 8), ((0, 9),), "zy"),
-    ((2, 6), ((20, 7), (60, 3)), "zy"),
+    ((2, 6), ((20, 7), (60, 3)), "xy"),
     ((3, 5), ((27, 4), (45, 6)), "yz"),
 )
 OWN = 44
-FIXED = 96
+FIXED = 80
 PAIRS = sum((n + 1) // 2 for _, ranges, _ in WAVES for _, n in ranges)
 
 SCHEDULE = (
-    ("G", 7), ("G", 1), (0, 0), ("G", 2), ("T", "late1"), ("T", "late0"), ("G", 6), (3, 0), (0, 1), ("G", 5),
-    ("G", 3), (4, 0), ("G", 8), (3, 1), (0, 2), ("G", 0), (2, 0), (4, 1), ("G", 4), (1, 0), ("A", 5), (2, 1),
-    (3, 2), ("A", 3), (1, 1), ("A", 6), (0, 3), ("A", 8), (2, 2), (4, 2), ("T", "hidden"), (1, 2), (3, 3),
-    (0, 4), (4, 3), ("T", "clip"), (0, 5), (1, 3), (2, 3), (3, 4), (4, 4), (1, 4), (2, 4), ("T", "out"),
-    (3, 5), (4, 5), (1, 5), (2, 5),
+    ("G", 1), ("G", 7), (0, 0), ("G", 4), (1, 0), ("T", "late1"), ("G", 5), ("G", 3), (4, 0), (0, 1),
+    ("T", "late0"), (1, 1), ("G", 6), ("G", 2), (3, 0), ("G", 0), (4, 1), ("A", 3), ("G", 8), (2, 0), (3, 1),
+    ("A", 8), (1, 2), ("A", 6), (2, 1), ("A", 5), (0, 2), ("T", "hidden"), (1, 3), (4, 2), (1, 4), (3, 2),
+    (0, 3), ("T", "clip"), (2, 2), (0, 4), (4, 3), (3, 3), (2, 3), (4, 4), ("T", "out"), (2, 4), (3, 4),
 )
 
 
@@ -73,7 +72,7 @@
     route, lengths, lat_in, cot_in, ink, bias_in, gain_in, ker_in,
     out_lat, out_wg,
     cotbuf, cot3, kbuf, tr1, tr2, stage, latg, lat4, s3, xt, hid, act, inv_ref, ag, hg, yt, lg, lgs, lgr, latg2,
-    gbuf, own, r1, r2, sb, q, fin, fr, outf,
+    gbuf, own, ra, sb, q, fin, fr, outf,
     local_sem, send_sem, recv_sem,
 ):
     clip, tile = lax.axis_index("clip"), lax.axis_index("tile")
@@ -115,6 +114,12 @@
     barrier = pltpu.get_barrier_semaphore()
     for p in peers:
         pl.semaphore_signal(barrier, inc=1, device_id=p, device_id_type=MESH)
+    def greet(p):
+        pl.semaphore_signal(barrier, inc=1, device_id=p, device_id_type=MESH)
+
+    for k in (1, 2, 3):
+        greet(at(clip=2 * z + core, tile=4 * ((z + k) % 4) + y))
+    pl.when(x != z)(lambda: greet(at(clip=2 * z + core, tile=4 * z + y)))
 
     lane16 = lax.broadcasted_iota(jnp.int32, (20, 128), 1) // LAT
     flat = jnp.concatenate([lat_in[j].astype(F32) for j in range(F)], axis=0)
@@ -128,7 +133,7 @@
         tr2[pl.ds(q8, 20, stride=8), :] = u
     pack(tr2[...].T.reshape(F, R * LAT, LANES), stage)
 
-    pl.semaphore_wait(barrier, len(peers))
+    pl.semaphore_wait(barrier, len(peers) + 3 + jnp.where(x != z, 1, 0))
 
     lat_g = [send(stage, latg.at[clip], d) for d in group]
     parts = (slice(2, 4), slice(1, 2), slice(0, 1))
@@ -250,13 +255,15 @@
         total = sum(n for _, n in ranges)
         mine = pl.ds(off, total)
         if order == "zy":
-            (a, ap, am), (b, bp, bm, bo) = (z, zp, zm), (y, yp, ym, yo)
+            (a, ap, am, ao), (b, bp, bm, bo) = (z, zp, zm, zo), (y, yp, ym, yo)
+        elif order == "yz":
+            (a, ap, am, ao), (b, bp, bm, bo) = (y, yp, ym, yo), (z, zp, zm, zo)
         else:
-            (a, ap, am), (b, bp, bm, bo) = (y, yp, ym), (z, zp, zm, zo)
+            (a, ap, am, ao), (b, bp, bm, bo) = (x, xp, xm, xo), (y, yp, ym, yo)
         st = {}
 
         def rows_a(k):
-            return 96 * ((a + k) % 4)
+            return pl.ds(pl.multiple_of(96 * ((a + k) % 4), 96), 96)
 
         def s0():
             st["c"], at0 = [], off
@@ -279,31 +286,19 @@
 
                 lax.fori_loop(0, n, body, 0, unroll=True)
                 at0 += n
-            r = pl.multiple_of(rows_a(2), 48)
-            st["p1"] = send(own.at[mine, pl.ds(r, 48)], r1.at[mine, 0], ap)
-            st["m1"] = send(own.at[mine, pl.ds(pl.multiple_of(r + 48, 48), 48)], r1.at[mine, 1], am)
+            st["a"] = [
+                send(own.at[mine, rows_a(k)], ra.at[mine, i], device)
+                for i, (k, device) in enumerate(((1, ap), (3, am), (2, ao)))
+            ]
 
         def s2():
-            for side, k, shift, device in ((0, 1, 0, ap), (1, 3, 48, am)):
-                st["pm"[side] + "1"].wait_recv()
-                rows = pl.ds(pl.multiple_of(rows_a(k) + shift, 48), 48)
-
-                def body(t, carry, rows=rows, side=side):
-                    own[off + t, rows] = own[off + t, rows] + r1[off + t, side]
-                    return carry
-
-                lax.fori_loop(0, total, body, 0, unroll=True)
-                st["pm"[side] + "2"] = send(
-                    own.at[mine, pl.ds(pl.multiple_of(rows_a(k), 96), 96)], r2.at[mine, side], device
-                )
-
-        def s3_():
-            st["p2"].wait_recv()
-            st["m2"].wait_recv()
-            rows = pl.ds(pl.multiple_of(rows_a(0), 96), 96)
+            for cp in st["a"]:
+                cp.wait_recv()
+            rows = rows_a(0)
 
             def block(i):
-                return own[i, rows].astype(F32) + r2[i, 0].astype(F32) + r2[i, 1].astype(F32)
+                v = own[i, rows].astype(F32) + ra[i, 0].astype(F32)
+                return v + ra[i, 1].astype(F32) + ra[i, 2].astype(F32)
 
             at0, p = off, poff
             for _, n in ranges:
@@ -321,7 +316,7 @@
                 for i, (k, device) in enumerate(((1, bp), (3, bm), (2, bo)))
             ]
 
-        def s4():
+        def s3_():
             for cp in st["q"]:
                 cp.wait_recv()
             p, st["owner"] = poff, []
@@ -333,38 +328,53 @@
                 mirror = 81 - first - n
                 owner = pick(first // 20, (mirror - 10) // 20)
                 base = FIXED + 4 * len(to_owner)
+                slot, to = (z, 4 * x + y) if order == "xy" else (x, tile)
                 cp = pltpu.make_async_remote_copy(
-                    src_ref=fin.at[pl.ds(p, count)], dst_ref=fr.at[x, pl.ds(p, count)],
-                    send_sem=send_sem.at[base], recv_sem=recv_sem.at[base + x],
-                    device_id=at(clip=2 * owner + core), device_id_type=MESH,
+                    src_ref=fin.at[pl.ds(p, count)], dst_ref=fr.at[slot, pl.ds(p, count)],
+                    send_sem=send_sem.at[base], recv_sem=recv_sem.at[base + slot],
+                    device_id=at(clip=2 * owner + core, tile=to), device_id_type=MESH,
                 )
-                to_owner.append((owner, cp))
+                away = (owner != x) | (to != tile)
+                to_owner.append((away, cp))
                 st["owner"].append((owner, base, p, n, pick(first % 20, (mirror - 10) % 20)))
-                pl.when(owner != x)(cp.start)
+                pl.when(away)(cp.start)
                 p += count
 
-        def s5():
+        def s4():
             for owner, base, p, n, place in st["owner"]:
 
                 @pl.when(owner == x)
                 def _(base=base, p=p, n=n, place=place):
                     count = (n + 1) // 2
-                    others_x = [(x + k) % 4 for k in (1, 3, 2)]
-                    for k in others_x:
+                    slot = z if order == "xy" else x
+                    others = [(slot + k) % 4 for k in (1, 3, 2)]
+                    mine = pl.ds(p, count)
+
+                    def arrive(k):
                         pltpu.make_async_remote_copy(
-                            src_ref=fin.at[pl.ds(p, count)], dst_ref=fr.at[k, pl.ds(p, count)],
+                            src_ref=fin.at[mine], dst_ref=fr.at[k, mine],
                             send_sem=send_sem.at[base], recv_sem=recv_sem.at[base + k],
                             device_id=xp, device_id_type=MESH,
                         ).wait_recv()
+
+                    for k in others:
+                        arrive(k)
+                    if order == "xy":
+                        pl.when(x != z)(lambda: arrive(z))
+
+                        @pl.when(x == z)
+                        def _():
+                            fr[z, mine] = fin[mine]
+
                     for i in range(count):
-                        v = fin[p + i].astype(F32)
-                        for k in others_x:
+                        v = (fr[z, p + i] if order == "xy" else fin[p + i]).astype(F32)
+                        for k in others:
                             v += fr[k, p + i].astype(F32)
                         outf[place + 2 * i] = v[:24]
                         if 2 * i + 1 < n:
                             outf[place + 2 * i + 1] = v[24:]
 
-        return [s0, s1, s2, s3_, s4, s5]
+        return [s0, s1, s2, s3_, s4]
 
     waves, off, poff = [], 0, 0
     for _, ranges, order in WAVES:
@@ -460,8 +470,8 @@
 
     for cp in copies:
         cp.wait_send()
-    for owner, cp in to_owner:
-        pl.when(owner != x)(cp.wait_send)
+    for away, cp in to_owner:
+        pl.when(away)(cp.wait_send)
 
 
 def on_device(latents, tile_route, lengths, reward_grad, in_kernel, in_bias, norm_gain, kernel_):
@@ -503,8 +513,7 @@
             v(CLIPS, F + 1, R * LAT, 128),
             v(81, C, 128),
             v(OWN, C, 128),
-            v(OWN, 2, 48, 128),
-            v(OWN, 2, 96, 128),
+            v(OWN, 3, 96, 128),
             v(4, PAIRS, 48, 128),
             v(3, PAIRS, 48, 128),
             v(PAIRS, 48, 128),

time: 76.2 us -> 72.7 us (0.954)
  Pallas kernels: 72.4 us -> 68.8 us
    pallas_call x1, Pallas kernels: 72.4 us -> 68.8 us  [on_device(): pl.pallas_call(kernel, out_shape=(jax.ShapeDtypeStruct((F, R, W * LAT), B...]
where the time goes in v5:
time: 72.7 us; the launch traced here: 72.5 us
  Pallas kernels  68.8 us (95%)
  local copies, waits for them, and re-layouts  3 us (4%)
    pallas_call x1, Pallas kernels, on_device(): pl.pallas_call(kernel, out_shape=(jax.ShapeDtypeStruct((F, R, W * LAT), B...  68.8 us
    unnamed x2, local copies, waits for them, and re-layouts  3 us

profile of v5, /device:TPU:0, one launch (start us, length us, event | category | flops | bytes accessed | tf_op | source)
XLA Modules:
  0.0 72.5 jit_solution(5858646852025196161)
XLA Ops:
  0.6 68.8 %backward.1 = (bf16[4,2,2560]{2,1,0:T(2,128)(2,1)}, f32[24,1296]{1,0:T(8,128)}) custom-call(s32[32]{0:T(128)} %route.1, s32[8]{0:T(128)} %lengths.1, bf16[4,2,2560]{2,1,0:T(2,128)(2,1)} %lat_in.1, bf16[1,4,2,160,384]{4,3,2,1,0:T(8,128)(2,1)} %cot_in.1, bf16[432,384]{1,0:T(8,128)(2,1)} %ink.1, f32[384]{0:T(512)} %bias_in.1, f32[384]{0:T(512)} %gain_in.1, ...), custom_call_target="tpu_custom_call" | custom-call | tf_op jit(solution)/shard_map/backward/pallas_call | solution.py:485
  69.5 1.4 %copy.12 = bf16[4,2,2560]{2,1,0:T(2,128)(2,1)} copy(bf16[4,2,2560]{2,1,0:T(2,128)(2,1)} %get-tuple-element.4) | data formatting | bytes 81920
  70.9 1.6 %copy.13 = f32[24,1296]{1,0:T(8,128)} copy(f32[24,1296]{1,0:T(8,128)} %get-tuple-element.5) | data formatting | bytes 248832

commit v6 on v5

--- a/solution.py
+++ b/solution.py
@@ -17,19 +17,19 @@
 WAVES = (
     ((1, 7), ((9, 2), (63, 8)), "zy"),
     ((4,), ((40, 5),), "yz"),
-    ((0, 8), ((0, 9),), "zy"),
-    ((2, 6), ((20, 7), (60, 3)), "xy"),
-    ((3, 5), ((27, 4), (45, 6)), "yz"),
+    ((0, 8), ((0, 9),), "yz"),
+    ((2, 6), ((20, 7), (60, 3)), "zy"),
+    ((3, 5), ((27, 4), (45, 6)), "xy"),
 )
 OWN = 44
 FIXED = 80
 PAIRS = sum((n + 1) // 2 for _, ranges, _ in WAVES for _, n in ranges)
 
 SCHEDULE = (
-    ("G", 1), ("G", 7), (0, 0), ("G", 4), (1, 0), ("T", "late1"), ("G", 5), ("G", 3), (4, 0), (0, 1),
-    ("T", "late0"), (1, 1), ("G", 6), ("G", 2), (3, 0), ("G", 0), (4, 1), ("A", 3), ("G", 8), (2, 0), (3, 1),
-    ("A", 8), (1, 2), ("A", 6), (2, 1), ("A", 5), (0, 2), ("T", "hidden"), (1, 3), (4, 2), (1, 4), (3, 2),
-    (0, 3), ("T", "clip"), (2, 2), (0, 4), (4, 3), (3, 3), (2, 3), (4, 4), ("T", "out"), (2, 4), (3, 4),
+    ("G", 1), ("G", 7), (0, 0), ("T", "late1"), ("T", "late0"), ("G", 8), ("G", 0), (2, 0), ("G", 5), (0, 1),
+    ("G", 3), (4, 0), ("G", 2), (2, 1), ("G", 6), (3, 0), ("G", 4), (1, 0), (4, 1), ("A", 6), ("A", 3),
+    (3, 1), (1, 1), ("A", 8), ("A", 5), ("T", "hidden"), (0, 2), (2, 2), (4, 2), (1, 2), ("T", "clip"),
+    (3, 2), (0, 3), (2, 3), (4, 3), (1, 3), (0, 4), (3, 3), (2, 4), ("T", "out"), (1, 4), (4, 4), (3, 4),
 )
 
 
@@ -474,6 +474,11 @@
         pl.when(away)(cp.wait_send)
 
 
+def hand_out(lat_in, wg_in, lat_out, wg_out):
+    lat_out[...] = lat_in[...]
+    wg_out[...] = wg_in[...]
+
+
 def on_device(latents, tile_route, lengths, reward_grad, in_kernel, in_bias, norm_gain, kernel_):
     vmem = pl.BlockSpec(memory_space=pltpu.VMEM)
     smem = pl.BlockSpec(memory_space=pltpu.SMEM)
@@ -482,7 +487,7 @@
     def v(*shape, dtype=BF):
         return pltpu.VMEM(shape, dtype)
 
-    return pl.pallas_call(
+    lat_grad, weight_grad = pl.pallas_call(
         kernel,
         out_shape=(
             jax.ShapeDtypeStruct((F, R, W * LAT), BF),
@@ -530,6 +535,16 @@
     )(
         tile_route, lengths, latents, reward_grad, in_kernel, in_bias, norm_gain, kernel_,
     )
+    return pl.pallas_call(
+        hand_out,
+        out_shape=(
+            jax.ShapeDtypeStruct(lat_grad.shape, BF),
+            jax.ShapeDtypeStruct(weight_grad.shape, F32),
+        ),
+        in_specs=[vmem, vmem],
+        out_specs=(vmem, vmem),
+        name="hand_out",
+    )(lat_grad, weight_grad)
 
 
 def solution(mesh):

time: 72.7 us -> 70.3 us (0.967)
  local copies, waits for them, and re-layouts: 3 us -> 0 us
    unnamed x2 -> x0, local copies, waits for them, and re-layouts: 3 us -> none
    pallas_call x0 -> x1, Pallas kernels: none -> 1.61 us  [on_device(): pl.pallas_call(hand_out, out_shape=(jax.ShapeDtypeStruct(lat_grad.shape,...]
    pallas_call x1, Pallas kernels: 68.8 us -> 67.2 us  [on_device(): pl.pallas_call(kernel, out_shape=(jax.ShapeDtypeStruct((F, R, W * LAT), B...]
where the time goes in v6:
time: 70.3 us; the launch traced here: 69.5 us
  Pallas kernels  68.8 us (98%)
    pallas_call x1, Pallas kernels, on_device(): pl.pallas_call(kernel, out_shape=(jax.ShapeDtypeStruct((F, R, W * LAT), B...  67.2 us
    pallas_call x1, Pallas kernels, on_device(): pl.pallas_call(hand_out, out_shape=(jax.ShapeDtypeStruct(lat_grad.shape,...  1.61 us

profile of v6, /device:TPU:0, one launch (start us, length us, event | category | flops | bytes accessed | tf_op | source)
XLA Modules:
  0.0 69.5 jit_solution(8297997756546442737)
XLA Ops:
  0.6 67.2 %backward.1 = (bf16[4,2,2560]{2,1,0:T(2,128)(2,1)}, f32[24,1296]{1,0:T(8,128)}) custom-call(s32[32]{0:T(128)} %route.1, s32[8]{0:T(128)} %lengths.1, bf16[4,2,2560]{2,1,0:T(2,128)(2,1)} %lat_in.1, bf16[1,4,2,160,384]{4,3,2,1,0:T(8,128)(2,1)} %cot_in.1, bf16[432,384]{1,0:T(8,128)(2,1)} %ink.1, f32[384]{0:T(512)} %bias_in.1, f32[384]{0:T(512)} %gain_in.1, ...), custom_call_target="tpu_custom_call" | custom-call | tf_op jit(solution)/shard_map/backward/pallas_call | solution.py:490
  67.9 1.6 %hand_out.1 = (bf16[4,2,2560]{2,1,0:T(2,128)(2,1)}, f32[24,1296]{1,0:T(8,128)}) custom-call(bf16[4,2,2560]{2,1,0:T(2,128)(2,1)} %get-tuple-element.4.lat_in, f32[24,1296]{1,0:T(8,128)} %get-tuple-element.5.wg_in), custom_call_target="tpu_custom_call" | custom-call | tf_op jit(solution)/shard_map/hand_out/pallas_call | solution.py:538

commit v7 on v6

--- a/solution.py
+++ b/solution.py
@@ -71,7 +71,7 @@
 def kernel(
     route, lengths, lat_in, cot_in, ink, bias_in, gain_in, ker_in,
     out_lat, out_wg,
-    cotbuf, cot3, kbuf, tr1, tr2, stage, latg, lat4, s3, xt, hid, act, inv_ref, ag, hg, yt, lg, lgs, lgr, latg2,
+    cotbuf, cot3, kbuf, tr1, tr2, stage, latg, lat4, s3, xt, hid, act, inv_ref, ag, yt, lg, lgs, lgr, latg2,
     gbuf, own, ra, sb, q, fin, fr, outf,
     local_sem, send_sem, recv_sem,
 ):
@@ -222,18 +222,15 @@
                     else:
                         xt[at_rows, at_cols] = jnp.zeros((48, W), BF)
     gain = as_column(gain_in)
-    hid[...] = dot(ink[...], xt[...], 0, 0) + as_column(bias_in)
-
-    def norm_step(n, carry):
-        cols = pl.ds(pl.multiple_of(n * 128, 128), 128)
-        h = hid[:, cols]
+    bias = as_column(bias_in)
+    for n in range(0, POS, 256):
+        cols = slice(n, n + 256)
+        h = dot(ink[...], xt[:, cols], 0, 0) + bias
+        hid[:, cols] = h
         inv = lax.rsqrt(jnp.mean(h * h, axis=0, keepdims=True) + EPS)
         normed = h * inv * gain
         act[:, cols] = (normed * sigmoid(normed)).astype(BF)
         inv_ref[:, cols] = inv
-        return carry
-
-    lax.fori_loop(0, POS // 128, norm_step, 0)
 
     def weight_part(g, order):
         dt, dy = g // 3, g % 3
@@ -384,18 +381,15 @@
     orders = {g: order for groups, _, order in WAVES for g in groups}
 
     def hidden_grad():
-        def grad_step(n, carry):
-            cols = pl.ds(pl.multiple_of(n * 128, 128), 128)
+        for n in range(0, POS, 256):
+            cols = slice(n, n + 256)
             h, inv = hid[:, cols], inv_ref[:, cols]
             normed = h * inv * gain
             s = sigmoid(normed)
             gained = ag[:, cols] * s * (1.0 + normed * (1.0 - s)) * gain
             inner = jnp.mean(gained * h, axis=0, keepdims=True)
-            hg[:, cols] = (inv * gained - h * (inv * inv * inv * inner)).astype(BF)
-            return carry
-
-        lax.fori_loop(0, POS // 128, grad_step, 0)
-        yt[...] = dot(ink[...], hg[...], 1, 0)
+            grad = (inv * gained - h * (inv * inv * inv * inner)).astype(BF)
+            yt[:, cols] = dot(ink[...], grad, 1, 0)
 
         col = lax.broadcasted_iota(jnp.int32, (LAT, POS), 1) % W
         summed = []
@@ -510,7 +504,6 @@
             v(C, POS),
             v(1, POS, dtype=F32),
             v(C, POS, dtype=F32),
-            v(C, POS),
             v(27 * LAT, POS, dtype=F32),
             v(F, 4, LAT, LANES, dtype=F32),
             v(2, F + 1, LAT, 128, dtype=F32),

time: 70.3 us -> 70 us (level)
  no operation moved by 1% of the time
where the time goes in v7:
time: 70 us; the launch traced here: 69.1 us
  Pallas kernels  68.5 us (98%)
    pallas_call x1, Pallas kernels, on_device(): pl.pallas_call(kernel, out_shape=(jax.ShapeDtypeStruct((F, R, W * LAT), B...  66.9 us
    pallas_call x1, Pallas kernels, on_device(): pl.pallas_call(hand_out, out_shape=(jax.ShapeDtypeStruct(lat_grad.shape,...  1.61 us

profile of v7, /device:TPU:0, one launch (start us, length us, event | category | flops | bytes accessed | tf_op | source)
XLA Modules:
  0.0 69.1 jit_solution(10559831093660290736)
XLA Ops:
  0.6 66.9 %backward.1 = (bf16[4,2,2560]{2,1,0:T(2,128)(2,1)}, f32[24,1296]{1,0:T(8,128)}) custom-call(s32[32]{0:T(128)} %route.1, s32[8]{0:T(128)} %lengths.1, bf16[4,2,2560]{2,1,0:T(2,128)(2,1)} %lat_in.1, bf16[1,4,2,160,384]{4,3,2,1,0:T(8,128)(2,1)} %cot_in.1, bf16[432,384]{1,0:T(8,128)(2,1)} %ink.1, f32[384]{0:T(512)} %bias_in.1, f32[384]{0:T(512)} %gain_in.1, ...), custom_call_target="tpu_custom_call" | custom-call | tf_op jit(solution)/shard_map/backward/pallas_call | solution.py:484
  67.5 1.6 %hand_out.1 = (bf16[4,2,2560]{2,1,0:T(2,128)(2,1)}, f32[24,1296]{1,0:T(8,128)}) custom-call(bf16[4,2,2560]{2,1,0:T(2,128)(2,1)} %get-tuple-element.4.lat_in, f32[24,1296]{1,0:T(8,128)} %get-tuple-element.5.wg_in), custom_call_target="tpu_custom_call" | custom-call | tf_op jit(solution)/shard_map/hand_out/pallas_call | solution.py:531

commit v8 on v7

--- a/solution.py
+++ b/solution.py
@@ -16,7 +16,7 @@
 
 WAVES = (
     ((1, 7), ((9, 2), (63, 8)), "zy"),
-    ((4,), ((40, 5),), "yz"),
+    ((4,), ((40, 5),), "xy"),
     ((0, 8), ((0, 9),), "yz"),
     ((2, 6), ((20, 7), (60, 3)), "zy"),
     ((3, 5), ((27, 4), (45, 6)), "xy"),

time: 70 us -> 71.7 us (1.024)
  the two profiles are of different devices: /device:TPU:0 before, /device:TPU:2 now
where the time goes in v8:
time: 71.7 us; the launch traced here: 71.5 us
  Pallas kernels  70.9 us (99%)
    pallas_call x1, Pallas kernels, on_device(): pl.pallas_call(kernel, out_shape=(jax.ShapeDtypeStruct((F, R, W * LAT), B...  69.3 us
    pallas_call x1, Pallas kernels, on_device(): pl.pallas_call(hand_out, out_shape=(jax.ShapeDtypeStruct(lat_grad.shape,...  1.61 us

profile of v8, /device:TPU:2, one launch (start us, length us, event | category | flops | bytes accessed | tf_op | source)
XLA Modules:
  0.0 71.5 jit_solution(17139950148700333559)
XLA Ops:
  0.6 69.3 %backward.1 = (bf16[4,2,2560]{2,1,0:T(2,128)(2,1)}, f32[24,1296]{1,0:T(8,128)}) custom-call(s32[32]{0:T(128)} %route.1, s32[8]{0:T(128)} %lengths.1, bf16[4,2,2560]{2,1,0:T(2,128)(2,1)} %lat_in.1, bf16[1,4,2,160,384]{4,3,2,1,0:T(8,128)(2,1)} %cot_in.1, bf16[432,384]{1,0:T(8,128)(2,1)} %ink.1, f32[384]{0:T(512)} %bias_in.1, f32[384]{0:T(512)} %gain_in.1, ...), custom_call_target="tpu_custom_call" | custom-call | tf_op jit(solution)/shard_map/backward/pallas_call | solution.py:484
  69.9 1.6 %hand_out.1 = (bf16[4,2,2560]{2,1,0:T(2,128)(2,1)}, f32[24,1296]{1,0:T(8,128)}) custom-call(bf16[4,2,2560]{2,1,0:T(2,128)(2,1)} %get-tuple-element.4.lat_in, f32[24,1296]{1,0:T(8,128)} %get-tuple-element.5.wg_in), custom_call_target="tpu_custom_call" | custom-call | tf_op jit(solution)/shard_map/hand_out/pallas_call | solution.py:531
